TPU v7x, 32 devices: a whole 2x2x4 slice. The times are simulated.
32 devices in a mesh: dp: 8 (over y, x, core), ctx: 4 (over z).
Axes of the slice: x: 2, y: 2, z: 4, core: 2. Of those that a mesh axis runs over, the one named last changes fastest.
Arguments:
- tokens: bfloat16 [8192, 960], P(('dp', 'ctx')), may hold values from -6 to 6
- w_query: bfloat16 [921600], P(('dp', 'ctx')), may hold values from -0.1875 to 0.1875
- w_key: bfloat16 [307200], P(('dp', 'ctx')), may hold values from -0.1875 to 0.1875
- w_value: bfloat16 [307200], P(('dp', 'ctx')), may hold values from -0.1875 to 0.1875
- w_out: bfloat16 [921600], P(('dp', 'ctx')), may hold values from -6 to 6
- w_gate: bfloat16 [2457600], P(('dp', 'ctx')), may hold values from -0.1875 to 0.1875
- w_up: bfloat16 [2457600], P(('dp', 'ctx')), may hold values from -0.1875 to 0.1875
- w_down: bfloat16 [2457600], P(('dp', 'ctx')), may hold values from -0.125 to 0.125
- norm_gains: bfloat16 [2, 960], P(None, 'dp'), may hold values from 0.5 to 1.5
- cotangent: bfloat16 [8192, 960], P(('dp', 'ctx')), may hold values from -6 to 6
Outputs:
- layer_out: bfloat16 [8192, 960], P(('dp', 'ctx'))
- grad_tokens: bfloat16 [8192, 960], P(('dp', 'ctx'))
- grad_query: float32 [921600], P(('dp', 'ctx'))
- grad_key: float32 [307200], P(('dp', 'ctx'))
- grad_value: float32 [307200], P(('dp', 'ctx'))
- grad_out: float32 [921600], P(('dp', 'ctx'))
- grad_gate: float32 [2457600], P(('dp', 'ctx'))
- grad_up: float32 [2457600], P(('dp', 'ctx'))
- grad_down: float32 [2457600], P(('dp', 'ctx'))
- grad_gains: float32 [2, 960], P(None, 'dp')
All inputs are finite; a program needn't handle non-finite values.
Results may differ from a plain program's by a relative error of at most 0.019.
Values may be sent and summed in bfloat16 or wider, within the bound.
A program may use at most 192 MiB of HBM per device.

v0:
```python
import math

import jax
import jax.numpy as jnp
from jax import lax
from jax.sharding import PartitionSpec as P

D = 960
FF = 2560
HEADS = 15
KV_HEADS = 5
HEAD_DIM = 64


EPSILON = 1e-05
THETA = 100000.0


def product(left, right):
    return jnp.dot(left, right, preferred_element_type=jnp.float32)


def product_left(left, right):
    return lax.dot_general(
        left, right, (((0,), (0,)), ((), ())), preferred_element_type=jnp.float32
    )


def product_right(left, right):
    return lax.dot_general(
        left, right, (((1,), (1,)), ((), ())), preferred_element_type=jnp.float32
    )


def flat_rows(left, right):
    block = product_left(left, right).reshape(-1)
    return block


def rope_tables(places):
    half = HEAD_DIM // 2
    frequency = THETA ** (-jnp.arange(half, dtype=jnp.float32) * 2.0 / HEAD_DIM)
    angle = places.astype(jnp.float32)[:, None] * frequency[None, :]
    return (jnp.cos(angle)[:, None, :], jnp.sin(angle)[:, None, :])


def rotate(values, cosine, sine, direction):
    half = HEAD_DIM // 2
    shaped = values.reshape(values.shape[0], -1, HEAD_DIM)
    first = shaped[..., :half]
    second = shaped[..., half:]
    turned = jnp.concatenate(
        [first * cosine - direction * second * sine, second * cosine + direction * first * sine],
        axis=-1,
    )
    return turned.reshape(values.shape)


def rms_forward(values, gain):
    factor = lax.rsqrt(jnp.mean(values * values, axis=-1, keepdims=True) + EPSILON)
    return (values * factor * gain, factor)


def rms_backward(values, factor, gain, grad):
    inner = grad * gain
    gain_grad = jnp.sum(grad * values * factor, axis=0)
    cube = factor * factor * factor
    input_grad = factor * inner - values * cube * jnp.mean(inner * values, axis=-1, keepdims=True)
    return (input_grad, gain_grad)


def per_device(tokens, w_query, w_key, w_value, w_out, w_gate, w_up, w_down, norm_gains, cotangent):
    local_rows = tokens.shape[0]
    query_width = HEADS * HEAD_DIM
    pair_width = KV_HEADS * HEAD_DIM
    groups = HEADS // KV_HEADS
    factor_scale = HEAD_DIM ** (-0.5)

    def shaped_attention(flats):
        return (
            flats[0].reshape(D, query_width),
            flats[1].reshape(D, pair_width),
            flats[2].reshape(D, pair_width),
            flats[3].reshape(query_width, D),
        )

    def shaped_feed(flats):
        return (flats[0].reshape(D, FF), flats[1].reshape(D, FF), flats[2].reshape(FF, D))

    attn_set = shaped_attention(
        (
            lax.all_gather(w_query, ("dp", "ctx"), axis=0, tiled=True),
            lax.all_gather(w_key, ("dp", "ctx"), axis=0, tiled=True),
            lax.all_gather(w_value, ("dp", "ctx"), axis=0, tiled=True),
            lax.all_gather(w_out, ("dp", "ctx"), axis=0, tiled=True),
        )
    )
    feed_set = shaped_feed(
        (
            lax.all_gather(w_gate, ("dp", "ctx"), axis=0, tiled=True),
            lax.all_gather(w_up, ("dp", "ctx"), axis=0, tiled=True),
            lax.all_gather(w_down, ("dp", "ctx"), axis=0, tiled=True),
        )
    )
    gains = lax.all_gather(norm_gains, "dp", axis=1, tiled=True).astype(jnp.float32)
    ctx_place = lax.axis_index("ctx")
    places = ctx_place * local_rows + jnp.arange(local_rows, dtype=jnp.int32)
    last_place = ctx_place * local_rows + local_rows - 1
    cosine, sine = rope_tables(places)
    inputs = tokens.astype(jnp.float32)
    scaled_first, rms_first = rms_forward(inputs, gains[0])
    normed_first = scaled_first.astype(jnp.bfloat16)
    query_matrix, key_matrix, value_matrix, out_matrix = attn_set
    query = rotate(product(normed_first, query_matrix), cosine, sine, 1.0).astype(jnp.bfloat16)
    key = rotate(product(normed_first, key_matrix), cosine, sine, 1.0).astype(jnp.bfloat16)
    value = product(normed_first, value_matrix).astype(jnp.bfloat16)
    pairs = jnp.concatenate([key, value], axis=1)
    query_heads = query.reshape(local_rows, KV_HEADS, groups, HEAD_DIM)
    start_state = (
        jnp.full((KV_HEADS, groups, local_rows), -1e30, jnp.float32),
        jnp.zeros((KV_HEADS, groups, local_rows), jnp.float32),
        jnp.zeros((KV_HEADS, groups, local_rows, HEAD_DIM), jnp.float32),
    )
    piece = lax.all_gather(pairs, "ctx", axis=0, tiled=True)
    count = piece.shape[0]
    fold_width = math.gcd(count, 512)

    def one_block(block_index, state):
        first_place = block_index * fold_width

        def compute(state_in):
            running_top, running_total, weighted = state_in
            block = lax.dynamic_slice_in_dim(piece, block_index * fold_width, fold_width, 0)
            key_block = block[:, :pair_width].reshape(fold_width, KV_HEADS, HEAD_DIM)
            value_block = block[:, pair_width:].reshape(fold_width, KV_HEADS, HEAD_DIM)
            scores = (
                jnp.einsum(
                    "qgrd,kgd->grqk", query_heads, key_block, preferred_element_type=jnp.float32
                )
                * factor_scale
            )
            key_places = first_place + jnp.arange(fold_width, dtype=jnp.int32)
            allowed = places[:, None] >= key_places[None, :]
            scores = jnp.where(allowed, scores, -1e30)
            new_top = jnp.maximum(running_top, jnp.max(scores, axis=-1))
            weights = jnp.exp(scores - new_top[..., None])
            decay = jnp.exp(running_top - new_top)
            new_total = running_total * decay + jnp.sum(weights, axis=-1)
            new_weighted = weighted * decay[..., None] + jnp.einsum(
                "grqk,kgd->grqd",
                weights.astype(jnp.bfloat16),
                value_block,
                preferred_element_type=jnp.float32,
            )
            return (new_top, new_total, new_weighted)

        def keep_state(state_in):
            return state_in

        return lax.cond(first_place <= last_place, compute, keep_state, state)

    final_top, final_total, weighted = lax.fori_loop(0, count // fold_width, one_block, start_state)
    mixed_heads = weighted / final_total[..., None]
    log_total = final_top + jnp.log(final_total)
    mixed_low = (
        mixed_heads.transpose(2, 0, 1, 3).reshape(local_rows, query_width).astype(jnp.bfloat16)
    )
    hidden = inputs + product(mixed_low, out_matrix)
    scaled_second, rms_second = rms_forward(hidden, gains[1])
    normed_second = scaled_second.astype(jnp.bfloat16)
    gate_matrix, up_matrix, down_matrix = feed_set
    gate_values = product(normed_second, gate_matrix)
    up_values = product(normed_second, up_matrix)
    sigmoid_gate = jax.nn.sigmoid(gate_values)
    silu_gate = gate_values * sigmoid_gate
    active = (silu_gate * up_values).astype(jnp.bfloat16)
    layer_out = (hidden + product(active, down_matrix)).astype(jnp.bfloat16)
    attn_set = shaped_attention(
        (
            lax.all_gather(w_query, ("dp", "ctx"), axis=0, tiled=True),
            lax.all_gather(w_key, ("dp", "ctx"), axis=0, tiled=True),
            lax.all_gather(w_value, ("dp", "ctx"), axis=0, tiled=True),
            lax.all_gather(w_out, ("dp", "ctx"), axis=0, tiled=True),
        )
    )
    feed_set = shaped_feed(
        (
            lax.all_gather(w_gate, ("dp", "ctx"), axis=0, tiled=True),
            lax.all_gather(w_up, ("dp", "ctx"), axis=0, tiled=True),
            lax.all_gather(w_down, ("dp", "ctx"), axis=0, tiled=True),
        )
    )
    query_matrix, key_matrix, value_matrix, out_matrix = attn_set
    gate_matrix, up_matrix, down_matrix = feed_set
    grad_layer = cotangent.astype(jnp.float32)
    grad_branch = grad_layer.astype(jnp.bfloat16)
    grad_active = product_right(grad_branch, down_matrix)
    grad_gate_values = (
        grad_active * up_values * (sigmoid_gate * (1.0 + gate_values * (1.0 - sigmoid_gate)))
    ).astype(jnp.bfloat16)
    grad_up_values = (grad_active * silu_gate).astype(jnp.bfloat16)
    grad_normed_second = product_right(grad_gate_values, gate_matrix) + product_right(
        grad_up_values, up_matrix
    )
    grad_hidden_norm, gain_second = rms_backward(hidden, rms_second, gains[1], grad_normed_second)
    grad_hidden = grad_layer + grad_hidden_norm
    grad_attn = grad_hidden.astype(jnp.bfloat16)
    grad_mixed = product_right(grad_attn, out_matrix).astype(jnp.bfloat16)
    grad_heads = grad_mixed.reshape(local_rows, KV_HEADS, groups, HEAD_DIM)
    delta = jnp.sum(grad_heads.astype(jnp.float32).transpose(1, 2, 0, 3) * mixed_heads, axis=-1)

    def block_grads(block, first_key):
        width = block.shape[0]
        key_block = block[:, :pair_width].reshape(width, KV_HEADS, HEAD_DIM)
        value_block = block[:, pair_width:].reshape(width, KV_HEADS, HEAD_DIM)
        scores = (
            jnp.einsum("qgrd,kgd->grqk", query_heads, key_block, preferred_element_type=jnp.float32)
            * factor_scale
        )
        key_places = first_key + jnp.arange(width, dtype=jnp.int32)
        allowed = places[:, None] >= key_places[None, :]
        scores = jnp.where(allowed, scores, -1e30)
        weights = jnp.exp(scores - log_total[..., None])
        grad_weights = jnp.einsum(
            "qgrd,kgd->grqk", grad_heads, value_block, preferred_element_type=jnp.float32
        )
        grad_scores = (weights * (grad_weights - delta[..., None])).astype(jnp.bfloat16)
        query_add = (
            jnp.einsum("grqk,kgd->grqd", grad_scores, key_block, preferred_element_type=jnp.float32)
            * factor_scale
        )
        grad_key_block = (
            jnp.einsum(
                "grqk,qgrd->kgd", grad_scores, query_heads, preferred_element_type=jnp.float32
            )
            * factor_scale
        )
        grad_value_block = jnp.einsum(
            "grqk,qgrd->kgd",
            weights.astype(jnp.bfloat16),
            grad_heads,
            preferred_element_type=jnp.float32,
        )
        piece = jnp.concatenate(
            [
                grad_key_block.reshape(width, pair_width),
                grad_value_block.reshape(width, pair_width),
            ],
            axis=1,
        )
        return (query_add, piece)

    query_zero = jnp.zeros((KV_HEADS, groups, local_rows, HEAD_DIM), jnp.float32)
    whole = lax.all_gather(pairs, "ctx", axis=0, tiled=True)
    width = math.gcd(whole.shape[0], max(local_rows, 512))

    def back_block(block_index, state):
        grad_query_heads, term = state
        block = lax.dynamic_slice_in_dim(whole, block_index * width, width, 0)
        query_add, piece = block_grads(block, block_index * width)
        term = lax.dynamic_update_slice_in_dim(term, piece, block_index * width, 0)
        return (grad_query_heads + query_add, term)

    start_back = (query_zero, jnp.zeros((whole.shape[0], 2 * pair_width), jnp.float32))
    grad_query_heads, term = lax.fori_loop(0, last_place // width + 1, back_block, start_back)
    pair_grads = lax.psum_scatter(
        term.astype(jnp.bfloat16), "ctx", scatter_dimension=0, tiled=True
    ).astype(jnp.float32)
    grad_query_rot = grad_query_heads.transpose(2, 0, 1, 3).reshape(local_rows, query_width)
    grad_query_lin = rotate(grad_query_rot, cosine, sine, -1.0).astype(jnp.bfloat16)
    grad_key_lin = rotate(pair_grads[:, :pair_width], cosine, sine, -1.0).astype(jnp.bfloat16)
    grad_value_lin = pair_grads[:, pair_width:].astype(jnp.bfloat16)
    grad_normed_first = (
        product_right(grad_query_lin, query_matrix)
        + product_right(grad_key_lin, key_matrix)
        + product_right(grad_value_lin, value_matrix)
    )
    grad_input_norm, gain_first = rms_backward(inputs, rms_first, gains[0], grad_normed_first)
    grad_tokens = (grad_hidden + grad_input_norm).astype(jnp.bfloat16)
    attn_lengths = (w_query.shape[0], w_key.shape[0], w_value.shape[0], w_out.shape[0])
    attn_pairs = (
        (normed_first, grad_query_lin),
        (normed_first, grad_key_lin),
        (normed_first, grad_value_lin),
        (mixed_low, grad_attn),
    )
    feed_lengths = (w_gate.shape[0], w_up.shape[0], w_down.shape[0])
    feed_pairs = (
        (normed_second, grad_gate_values),
        (normed_second, grad_up_values),
        (active, grad_branch),
    )
    pieces = [
        flat_rows(left, right).reshape(1 * lax.axis_size(("dp", "ctx")), size)
        for (left, right), size in zip(attn_pairs, attn_lengths)
    ]
    attn_row = lax.psum_scatter(
        jnp.concatenate(pieces, axis=1), ("dp", "ctx"), scatter_dimension=0, tiled=True
    )[0]
    pieces = [
        flat_rows(left, right).reshape(1 * lax.axis_size(("dp", "ctx")), size)
        for (left, right), size in zip(feed_pairs, feed_lengths)
    ]
    feed_row = lax.psum_scatter(
        jnp.concatenate(pieces, axis=1), ("dp", "ctx"), scatter_dimension=0, tiled=True
    )[0]
    attn_cuts = [sum(attn_lengths[:index]) for index in range(5)]
    feed_cuts = [sum(feed_lengths[:index]) for index in range(4)]
    attn_grads = [attn_row[attn_cuts[index] : attn_cuts[index + 1]] for index in range(4)]
    feed_grads = [feed_row[feed_cuts[index] : feed_cuts[index + 1]] for index in range(3)]
    gain_part = lax.psum_scatter(
        jnp.stack([gain_first, gain_second]), "dp", scatter_dimension=1, tiled=True
    )
    gain_total = lax.psum(gain_part, "ctx")
    return (
        layer_out,
        grad_tokens,
        attn_grads[0],
        attn_grads[1],
        attn_grads[2],
        attn_grads[3],
        feed_grads[0],
        feed_grads[1],
        feed_grads[2],
        gain_total,
    )


def solution(mesh):
    placed = (
        P(("dp", "ctx"), None),
        P(("dp", "ctx")),
        P(("dp", "ctx")),
        P(("dp", "ctx")),
        P(("dp", "ctx")),
        P(("dp", "ctx")),
        P(("dp", "ctx")),
        P(("dp", "ctx")),
        P(None, "dp"),
        P(("dp", "ctx"), None),
    )
    return jax.shard_map(
        per_device,
        mesh=mesh,
        in_specs=placed,
        out_specs=(
            P(("dp", "ctx"), None),
            P(("dp", "ctx"), None),
            P(("dp", "ctx")),
            P(("dp", "ctx")),
            P(("dp", "ctx")),
            P(("dp", "ctx")),
            P(("dp", "ctx")),
            P(("dp", "ctx")),
            P(("dp", "ctx")),
            P(None, "dp"),
        ),
        check_vma=False,
    )
```

profile of v0, /device:TPU:0, one launch (start us, length us, event | category | flops | bytes accessed | tf_op | source)
XLA Modules:
  0.0 1166.7 jit_solution(14268007268510877001)
XLA Ops:
  10.4 10.3 all-gather
  22.4 84.9 %all-gather.2 = bf16[32,1,9600]{2,1,0:T(2,128)(2,1)S(1)} all-gather(bf16[1,1,9600]{2,1,0:T(2,128)(2,1)S(1)} %reshape.238), channel_id=1, replica_groups=mesh['dp'=8,'ctx'=4] {'dp','ctx'}, dimensions={0}, use_global_device_ids=true | all-gather | bytes 633600 | tf_op jit(solution)/shard_map/all_gather | solution.py:94
  111.8 79.8 %all-gather.1 = bf16[32,1,9600]{2,1,0:T(2,128)(2,1)S(1)} all-gather(bf16[1,1,9600]{2,1,0:T(2,128)(2,1)S(1)} %reshape.236), channel_id=1, replica_groups=mesh['dp'=8,'ctx'=4] {'dp','ctx'}, dimensions={0}, use_global_device_ids=true | all-gather | bytes 633600 | tf_op jit(solution)/shard_map/all_gather | solution.py:93
  191.6 4.5 reduce
  205.8 39.6 %reduce.3 = bf16[32,28800]{1,0:T(8,128)(2,1)S(1)} reduce(bf16[32,1,28800]{2,1,0:T(2,128)(2,1)} %all-gather.22.cloned.1.call-done, bf16[]{:T(256)} %constant.108), dimensions={1}, to_apply=%all-gather.4.reduce_sub_computation | reduce | bytes 3686402 | tf_op jit(solution)/shard_map/all_gather | solution.py:95
  248.1 40.8 %reduce.2 = bf16[32,28800]{1,0:T(8,128)(2,1)} reduce(bf16[32,1,28800]{2,1,0:T(2,128)(2,1)} %all-gather.20.cloned.1.call-done, bf16[]{:T(256)} %constant.108), dimensions={1}, to_apply=%all-gather.3.reduce_sub_computation | reduce | bytes 3686402 | tf_op jit(solution)/shard_map/all_gather | solution.py:92
  297.3 7.1 while.31
  297.8 6.5 conditional.3
  307.7 10.1 reshape.226
  317.8 46.8 %all-gather.16.cloned.1.call-done = bf16[2457600]{0:T(1024)(128)(2,1)} async-done(((bf16[76800]{0:T(1024)(128)(2,1)}), bf16[2457600]{0:T(1024)(128)(2,1)}) %all-gather.16.cloned.1.call-update) | async-done | bytes 4915216 | tf_op jit(solution)/shard_map/all_gather | solution.py:101
  364.6 10.0 reshape.227
  374.6 5.7 fusion.65
  383.3 47.1 %all-gather.18.cloned.1.call-done = bf16[2457600]{0:T(1024)(128)(2,1)} async-done(((bf16[76800]{0:T(1024)(128)(2,1)}), bf16[2457600]{0:T(1024)(128)(2,1)}) %all-gather.18.cloned.1.call-update) | async-done | bytes 4915216 | tf_op jit(solution)/shard_map/all_gather | solution.py:102
  430.4 9.7 reshape.228
  440.2 7.6 multiply_convert_fusion
  447.7 3.9 fusion.66
  451.6 5.2 fusion.67
  456.9 5.2 fusion.68
  466.5 10.1 while.32
  476.7 10.3 reshape_reshape.30
  487.0 10.4 reshape_reshape.29
  497.4 5.6 fusion.69
  503.0 10.7 reshape_reshape.31
  513.7 21.1 %pad_maximum_fusion = f32[32,230400]{1,0:T(8,128)} fusion(f32[32,76800]{1,0:T(8,128)} %reshape_reshape.31, f32[32,76800]{1,0:T(8,128)} %reshape_reshape.30, f32[32,76800]{1,0:T(8,128)} %reshape_reshape.29), kind=kLoop, calls=%fused_computation.38 | loop fusion | flops 14745600 | bytes 58982400 | tf_op jit(solution)/shard_map/concatenate | solution.py:305
  537.4 5.2 reshape_reshape.28
  545.3 5.3 reshape_reshape.25
  562.1 6.7 pad_maximum_fusion.1
  573.1 5.6 fusion.28
  579.7 14.1 %all-reduce.2 = f32[2,960]{1,0:T(2,128)S(1)} all-reduce(f32[2,960]{1,0:T(2,128)S(1)} %pad_maximum_fusion.5), channel_id=5, replica_groups=mesh['dp'=8,'ctx'=4] {'dp'}, use_global_device_ids=true, to_apply=%region_18.19.clone | all-reduce | flops 1920 | bytes 15360
  593.9 21.7 %psum.7 = f32[2,120]{1,0:T(2,128)} all-reduce(f32[2,120]{1,0:T(2,128)S(1)} %constant_dynamic-slice_fusion.3), channel_id=1, replica_groups=mesh['dp'=8,'ctx'=4] {'ctx'}, use_global_device_ids=true, to_apply=%region_19.20 | all-reduce | flops 240 | bytes 1920 | tf_op jit(solution)/shard_map/psum | solution.py:314
  616.6 532.5 %all-reduce.6.cloned.1.call-done = (f32[32,76800]{1,0:T(8,128)}, f32[32,230400]{1,0:T(8,128)}) async-done(((f32[32,76800]{1,0:T(8,128)}, f32[32,230400]{1,0:T(8,128)}), (f32[32,76800]{1,0:T(8,128)}, f32[32,230400]{1,0:T(8,128)})) %all-reduce.6.cloned.1.call-update) | async-done | bytes 39321616
  1154.0 5.4 fusion.61
  (184 shorter events, 84.2 us)
Async XLA Ops:
  7.2 198.6 %all-gather.22.cloned.1.call-start = ((), (), s32[]{:S(2)}) async-start(), calls=%async_computation.7 | async-start | bytes 3801600 | tf_op jit(solution)/shard_map/all_gather | solution.py:95
  8.8 239.3 %all-gather.20.cloned.1.call-start = ((), (), s32[]{:S(2)}) async-start(), calls=%async_computation.6 | async-start | bytes 3801600 | tf_op jit(solution)/shard_map/all_gather | solution.py:92
  10.4 286.7 %all-gather.12.cloned.1.call-start = ((), (), s32[]{:S(2)}) async-start(), calls=%async_computation.1 | async-start | bytes 1638400 | tf_op jit(solution)/shard_map/all_gather | solution.py:124
  110.9 88.2 %copy-start.2 = (bf16[256,960]{0,1:T(8,128)(2,1)S(1)}, bf16[256,960]{0,1:T(8,128)(2,1)}, u32[]{:S(2)}) copy-start(bf16[256,960]{0,1:T(8,128)(2,1)} %param.16) | copy-start | bytes 1474564
  111.7 90.6 %copy-start.16 = (bf16[960,320]{1,0:T(8,128)(2,1)}, bf16[960,320]{1,0:T(8,128)(2,1)S(1)}, u32[]{:S(2)}) copy-start(bf16[960,320]{1,0:T(8,128)(2,1)S(1)} %reshape.223) | copy-start | bytes 1843204
  197.9 7.5 copy-start.10
  199.8 94.7 %copy-start.31 = (f32[256]{0:T(256)}, f32[256]{0:T(256)S(1)}, u32[]{:S(2)}) copy-start(f32[256]{0:T(256)S(1)} %get-tuple-element.372) | copy-start | bytes 3076
  199.9 94.7 %copy-start.29 = (f32[1,960]{1,0:T(1,128)}, f32[1,960]{1,0:T(1,128)S(1)}, u32[]{:S(2)}) copy-start(f32[1,960]{1,0:T(1,128)S(1)} %get-tuple-element.367) | copy-start | bytes 11524
  200.7 96.2 %copy-start.25 = (f32[256,32]{0,1:T(8,128)}, f32[256,32]{0,1:T(8,128)S(1)}, u32[]{:S(2)}) copy-start(f32[256,32]{0,1:T(8,128)S(1)} %get-tuple-element.370) | copy-start | bytes 98308
  203.7 104.0 %all-gather.14.cloned.1.call-start = ((), (), s32[]{:S(2)}) async-start(), calls=%async_computation.2 | async-start | bytes 5068800 | tf_op jit(solution)/shard_map/all_gather | solution.py:100
  204.3 160.3 %all-gather.16.cloned.1.call-start = ((), (), s32[]{:S(2)}) async-start(), calls=%async_computation.3 | async-start | bytes 5068800 | tf_op jit(solution)/shard_map/all_gather | solution.py:101
  204.9 225.6 %all-gather.18.cloned.1.call-start = ((), (), s32[]{:S(2)}) async-start(), calls=%async_computation.4 | async-start | bytes 5068800 | tf_op jit(solution)/shard_map/all_gather | solution.py:102
  205.5 345.3 %reduce-scatter.3.cloned.1.call-start = ((), (), s32[]{:S(2)}) async-start(), calls=%async_computation.5 | async-start | bytes 1638400 | tf_op jit(solution)/shard_map/reduce_scatter | solution.py:266
  304.4 13.4 %copy-start.6 = (f32[5,3,256,64]{2,3,1,0:T(8,128)}, f32[5,3,256,64]{2,3,1,0:T(8,128)S(1)}, u32[]{:S(2)}) copy-start(f32[5,3,256,64]{2,3,1,0:T(8,128)S(1)} %get-tuple-element.244) | copy-start | bytes 2949124
  307.4 156.3 %copy-start.14 = (f32[256,960]{0,1:T(8,128)}, f32[256,960]{0,1:T(8,128)S(1)}, u32[]{:S(2)}) copy-start(f32[256,960]{0,1:T(8,128)S(1)} %get-tuple-element.376) | copy-start | bytes 2949124
  374.5 5.7 copy-start
  383.3 56.9 %copy-start.18 = (bf16[256,960]{0,1:T(8,128)(2,1)S(1)}, bf16[256,960]{0,1:T(8,128)(2,1)}, u32[]{:S(2)}) copy-start(bf16[256,960]{0,1:T(8,128)(2,1)} %param.25) | copy-start | bytes 1474564
  451.6 10.4 slice-start
  456.8 5.2 slice-start.1
  476.6 672.6 %all-reduce.6.cloned.1.call-start = ((), (), s32[]{:S(2)}) async-start(), calls=%async_computation.8 | async-start | bytes 78643200
  487.0 10.4 copy-start.23
  513.7 21.1 %copy-start.5 = (f32[256,960]{0,1:T(8,128)S(1)}, f32[256,960]{0,1:T(8,128)}, u32[]{:S(2)}) copy-start(f32[256,960]{0,1:T(8,128)} %copy-done.4) | copy-start | bytes 2949124
  513.7 21.1 %copy-start.22 = (bf16[5,3,256,64]{2,3,1,0:T(8,128)(2,1)S(1)}, bf16[5,3,256,64]{2,3,1,0:T(8,128)(2,1)}, u32[]{:S(2)}) copy-start(bf16[5,3,256,64]{2,3,1,0:T(8,128)(2,1)} %copy-done.21) | copy-start | bytes 1474564
  537.3 5.2 copy-start.26
  537.3 5.2 copy-start.28
  537.3 5.4 copy-start.3
  537.3 5.4 copy-start.30
  537.3 5.4 copy-start.32
  573.0 5.6 copy-start.11
  573.1 6.0 copy-start.17
  573.1 6.0 copy-start.27
  578.6 37.0 %copy-start.33 = (f32[256]{0:T(256)S(1)}, f32[256]{0:T(256)}, u32[]{:S(2)}) copy-start(f32[256]{0:T(256)} %get-tuple-element.371) | copy-start | bytes 3076
  (13 other events, 27.3 us)
Sparse Core Ops, SparseCore 0:
  11.4 66.5 all-gather.21
  81.5 62.7 all-gather.19
  203.8 29.3 all-gather.11
  235.9 62.8 all-gather.13
  301.4 63.1 all-gather.15
  367.3 63.1 all-gather.17
  476.7 39.9 reduce-scatter.2
  568.9 580.1 all-reduce.5
where the time goes:
time: 1170 us
  waiting for transfers between devices  628 us (54%)
  blocking collectives  211 us (18%)
  other arithmetic  123 us (11%)
  local copies, waits for them, and re-layouts  112 us (10%)
  matrix products  75.5 us (6%)
  between operations  15.9 us (1%)
    unnamed x9, waiting for transfers between devices  534 us
    all_gather x1, blocking collectives, per_device(): lax.all_gather(w_value, ('dp', 'ctx'), axis=0, tiled=True)  84.9 us
    all_gather x1, blocking collectives, per_device(): lax.all_gather(w_key, ('dp', 'ctx'), axis=0, tiled=True)  79.8 us
    another operation x7, local copies, waits for them, and re-layouts, per_device(): flat_rows(left, right).reshape(1 * lax.axis_size(('dp', 'ctx')), size)  48.2 us
    all_gather x1, waiting for transfers between devices, per_device(): lax.all_gather(w_down, ('dp', 'ctx'), axis=0, tiled=True)  47.1 us
    all_gather x1, waiting for transfers between devices, per_device(): lax.all_gather(w_up, ('dp', 'ctx'), axis=0, tiled=True)  46.8 us
    all_gather x1, other arithmetic, per_device(): lax.all_gather(w_query, ('dp', 'ctx'), axis=0, tiled=True)  40.8 us
    all_gather x1, other arithmetic, per_device(): lax.all_gather(w_out, ('dp', 'ctx'), axis=0, tiled=True)  39.6 us
  transfers between devices with their start and end apart: 8, of which 3 were waited for; matrix products, arithmetic and copies ran while one was open for 20% of the time, Pallas kernels for 0%

commit v1 on v0

v1 whole, which is shorter than its diff:
```python
import functools

import jax
import jax.numpy as jnp
from jax import lax
from jax.sharding import PartitionSpec as P

D = 960
FF = 2560
HEADS = 15
KV_HEADS = 5
HEAD_DIM = 64


EPSILON = 1e-05
THETA = 100000.0


def product(left, right):
    return jnp.dot(left, right, preferred_element_type=jnp.float32)


def product_left(left, right):
    return lax.dot_general(
        left, right, (((0,), (0,)), ((), ())), preferred_element_type=jnp.float32
    )


def product_right(left, right):
    return lax.dot_general(
        left, right, (((1,), (1,)), ((), ())), preferred_element_type=jnp.float32
    )


LOW = jnp.bfloat16
BOTH = ("dp", "ctx")


def swap(values, axis, size, mask):
    return lax.ppermute(values, axis, [(index, index ^ mask) for index in range(size)])


def bits_of(size):
    return [1 << place for place in range(size.bit_length() - 1)]


class Exchange:
    def __init__(self, dp_size, ctx_size, dp_bits):
        stages = [("ctx", mask) for mask in reversed(bits_of(ctx_size))]
        stages += [("dp", mask) for mask in dp_bits] + [("dp", 1)]
        self.stages = stages
        self.sizes = {"dp": dp_size, "ctx": ctx_size}
        self.count = dp_size * ctx_size
        slots = jnp.arange(self.count, dtype=jnp.int32)
        place = {"dp": lax.axis_index("dp"), "ctx": lax.axis_index("ctx")}
        for index, (axis, mask) in enumerate(stages):
            place[axis] = place[axis] ^ (((slots >> index) & 1) * mask)
        self.shard = place["dp"] * ctx_size + place["ctx"]

    def gather(self, block):
        for axis, mask in self.stages:
            block = jnp.concatenate([block, swap(block, axis, self.sizes[axis], mask)], axis=0)
        return block

    def scatter(self, keep, send):
        for index, (axis, mask) in enumerate(reversed(self.stages)):
            got = swap(send.astype(LOW), axis, self.sizes[axis], mask)
            total = keep.astype(jnp.float32) + got.astype(jnp.float32)
            half = total.shape[0] // 2
            if index < len(self.stages) - 1:
                total = total.astype(LOW)
                keep, send = total[:half], total[half:]
        return total

    def selection(self, rows, padded):
        column = jnp.arange(padded, dtype=jnp.int32)
        source = jnp.where(column < rows, self.shard[:, None] * rows + column, -1).reshape(-1)
        feature = jnp.arange(self.count * rows, dtype=jnp.int32)
        return (feature[:, None] == source[None, :]).astype(LOW)


class RowWeights:
    def __init__(self, exchange, rows):
        self.exchange, self.rows = exchange, rows
        self.padded = -(-rows // 16) * 16
        self.select = exchange.selection(rows, self.padded)

    def gather(self, flats, widths):
        block = jnp.concatenate(
            [flat.reshape(self.rows, width) for flat, width in zip(flats, widths)], axis=1
        )
        return self.exchange.gather(jnp.pad(block, ((0, self.padded - self.rows), (0, 0))))

    def spread(self, values):
        return product(values, self.select).astype(LOW)

    def unspread(self, values):
        upper = values.astype(LOW)
        lower = (values - upper.astype(jnp.float32)).astype(LOW)
        return product_right(upper, self.select) + product_right(lower, self.select)

    def scatter(self, left, right, widths):
        half = left.shape[1] // 2
        send = product_left(left[:, half:], right).astype(LOW)
        total = self.exchange.scatter(product_left(left[:, :half], right), send)[: self.rows]
        cuts = [sum(widths[:index]) for index in range(len(widths) + 1)]
        return [total[:, low:high].reshape(-1) for low, high in zip(cuts[:-1], cuts[1:])]


class FlatWeights:
    def gather(self, flats, widths):
        return jnp.concatenate(
            [
                lax.all_gather(flat, BOTH, axis=0, tiled=True).reshape(-1, width)
                for flat, width in zip(flats, widths)
            ],
            axis=1,
        )

    def spread(self, values):
        return values.astype(LOW)

    def unspread(self, values):
        return values

    def scatter(self, left, right, widths):
        cuts = [sum(widths[:index]) for index in range(len(widths) + 1)]
        return [
            lax.psum_scatter(
                product_left(left, right[:, low:high]).astype(LOW).reshape(-1),
                BOTH,
                scatter_dimension=0,
                tiled=True,
            ).astype(jnp.float32)
            for low, high in zip(cuts[:-1], cuts[1:])
        ]


def rope_tables(places):
    half = HEAD_DIM // 2
    frequency = THETA ** (-jnp.arange(half, dtype=jnp.float32) * 2.0 / HEAD_DIM)
    angle = places.astype(jnp.float32)[:, None] * frequency[None, :]
    return (jnp.cos(angle)[:, None, :], jnp.sin(angle)[:, None, :])


def rotate(values, cosine, sine, direction):
    half = HEAD_DIM // 2
    shaped = values.reshape(values.shape[0], -1, HEAD_DIM)
    first = shaped[..., :half]
    second = shaped[..., half:]
    turned = jnp.concatenate(
        [first * cosine - direction * second * sine, second * cosine + direction * first * sine],
        axis=-1,
    )
    return turned.reshape(values.shape)


def rms_forward(values, gain):
    factor = lax.rsqrt(jnp.mean(values * values, axis=-1, keepdims=True) + EPSILON)
    return (values * factor * gain, factor)


def rms_backward(values, factor, gain, grad):
    inner = grad * gain
    gain_grad = jnp.sum(grad * values * factor, axis=0)
    cube = factor * factor * factor
    input_grad = factor * inner - values * cube * jnp.mean(inner * values, axis=-1, keepdims=True)
    return (input_grad, gain_grad)


def per_device(
    dp_size,
    ctx_size,
    tokens,
    w_query,
    w_key,
    w_value,
    w_out,
    w_gate,
    w_up,
    w_down,
    norm_gains,
    cotangent,
):
    local_rows = tokens.shape[0]
    query_width = HEADS * HEAD_DIM
    pair_width = KV_HEADS * HEAD_DIM
    groups = HEADS // KV_HEADS
    scale = HEAD_DIM ** (-0.5)
    devices = dp_size * ctx_size
    by_rows = D % devices == 0 and FF % devices == 0

    qkv_widths = (query_width, pair_width, pair_width)
    if by_rows:
        dp_bits = bits_of(dp_size)[1:]
        exchange_up = Exchange(dp_size, ctx_size, dp_bits)
        exchange_down = Exchange(dp_size, ctx_size, dp_bits[::-1])
        attn = RowWeights(exchange_up, D // devices)
        feed = RowWeights(exchange_down, D // devices)
        last_rows = FF // devices
    else:
        attn = feed = FlatWeights()

    gains = lax.all_gather(norm_gains, "dp", axis=1, tiled=True).astype(jnp.float32)
    qkv_matrix = attn.gather((w_query, w_key, w_value), qkv_widths)
    out_matrix = attn.gather((w_out,), (D,))
    feed_matrix = feed.gather((w_gate, w_up), (FF, FF))
    if by_rows:
        slots = exchange_up.gather(w_down.reshape(1, last_rows, D))
        down_matrix = jnp.take(slots, jnp.argsort(exchange_up.shard), axis=0).reshape(FF, D)
    else:
        down_matrix = feed.gather((w_down,), (D,))

    ctx_place = lax.axis_index("ctx")
    inner = jnp.arange(local_rows, dtype=jnp.int32)
    places = ctx_place * local_rows + inner
    others = ctx_place ^ jnp.arange(ctx_size, dtype=jnp.int32)
    key_places = (others[:, None] * local_rows + inner[None, :]).reshape(-1)
    cosine, sine = rope_tables(places)

    inputs = tokens.astype(jnp.float32)
    scaled_first, rms_first = rms_forward(inputs, gains[0])
    normed_first = attn.spread(scaled_first.astype(LOW))
    projected = product(normed_first, qkv_matrix)
    query = rotate(projected[:, :query_width], cosine, sine, 1.0).astype(LOW)
    key = rotate(projected[:, query_width : query_width + pair_width], cosine, sine, 1.0)
    pairs = jnp.concatenate([key.astype(LOW), projected[:, query_width + pair_width :].astype(LOW)], 1)
    whole = jnp.concatenate(
        [pairs] + [swap(pairs, "ctx", ctx_size, mask) for mask in range(1, ctx_size)], axis=0
    )
    count = whole.shape[0]

    def by_head(values):
        shaped = values.reshape(local_rows, KV_HEADS, groups, HEAD_DIM).transpose(1, 2, 0, 3)
        return shaped.reshape(KV_HEADS, groups * local_rows, HEAD_DIM)

    def by_token(values):
        shaped = values.reshape(KV_HEADS, groups, local_rows, HEAD_DIM).transpose(2, 0, 1, 3)
        return shaped.reshape(local_rows, query_width)

    def batched(pattern, left, right):
        return jnp.einsum(pattern, left, right, preferred_element_type=jnp.float32)

    query_heads = by_head(query)
    key_heads = whole[:, :pair_width].reshape(count, KV_HEADS, HEAD_DIM).transpose(1, 0, 2)
    value_heads = whole[:, pair_width:].reshape(count, KV_HEADS, HEAD_DIM).transpose(1, 0, 2)
    allowed = jnp.tile(places, groups)[:, None] >= key_places[None, :]
    scores = batched("gqd,gkd->gqk", query_heads, key_heads) * scale
    scores = jnp.where(allowed[None], scores, -1e30)
    top = jnp.max(scores, axis=-1, keepdims=True)
    unscaled = jnp.exp(scores - top)
    weights = unscaled * (1.0 / jnp.sum(unscaled, axis=-1, keepdims=True))
    weights_low = weights.astype(LOW)
    mixed_heads = batched("gqk,gkd->gqd", weights_low, value_heads)
    mixed_low = attn.spread(by_token(mixed_heads.astype(LOW)))

    hidden = inputs + product(mixed_low, out_matrix)
    scaled_second, rms_second = rms_forward(hidden, gains[1])
    normed_second = feed.spread(scaled_second.astype(LOW))
    gate_up = product(normed_second, feed_matrix)
    gate_values, up_values = gate_up[:, :FF], gate_up[:, FF:]
    sigmoid_gate = jax.nn.sigmoid(gate_values)
    silu_gate = gate_values * sigmoid_gate
    active = (silu_gate * up_values).astype(LOW)
    layer_out = (hidden + product(active, down_matrix)).astype(LOW)

    if by_rows:
        blocks = product_left(active, cotangent).astype(LOW).reshape(devices, last_rows, D)
        blocks = jnp.take(blocks, exchange_up.shard, axis=0)
        grad_down = exchange_up.scatter(blocks[: devices // 2], blocks[devices // 2 :]).reshape(-1)
    else:
        (grad_down,) = feed.scatter(active, cotangent, (D,))
    grad_layer = cotangent.astype(jnp.float32)
    grad_active = product_right(cotangent, down_matrix)
    grad_gate_values = grad_active * up_values * (
        sigmoid_gate * (1.0 + gate_values * (1.0 - sigmoid_gate))
    )
    grad_feed = jnp.concatenate(
        [grad_gate_values.astype(LOW), (grad_active * silu_gate).astype(LOW)], axis=1
    )
    grad_gate, grad_up = feed.scatter(normed_second, grad_feed, (FF, FF))
    grad_normed_second = feed.unspread(product_right(grad_feed, feed_matrix))
    grad_hidden_norm, gain_second = rms_backward(hidden, rms_second, gains[1], grad_normed_second)
    grad_hidden = grad_layer + grad_hidden_norm
    grad_attn = grad_hidden.astype(LOW)
    (grad_out,) = attn.scatter(mixed_low, grad_attn, (D,))
    grad_mixed = attn.unspread(product_right(grad_attn, out_matrix)).astype(LOW)

    grad_heads = by_head(grad_mixed)
    delta = jnp.sum(grad_heads.astype(jnp.float32) * mixed_heads, axis=-1, keepdims=True)
    grad_weights = batched("gqd,gkd->gqk", grad_heads, value_heads)
    grad_scores = (weights * (grad_weights - delta)).astype(LOW)
    grad_key_all = batched("gqk,gqd->gkd", grad_scores, query_heads) * scale
    grad_value_all = batched("gqk,gqd->gkd", weights_low, grad_heads)
    grad_query_heads = batched("gqk,gkd->gqd", grad_scores, key_heads) * scale
    term = jnp.concatenate([grad_key_all, grad_value_all], axis=0)
    term = term.transpose(1, 0, 2).reshape(ctx_size, local_rows, 2 * pair_width)
    pair_grads = term[0]
    for mask in range(1, ctx_size):
        pair_grads += swap(term[mask].astype(LOW), "ctx", ctx_size, mask).astype(jnp.float32)
    grad_projected = jnp.concatenate(
        [
            rotate(by_token(grad_query_heads), cosine, sine, -1.0).astype(LOW),
            rotate(pair_grads[:, :pair_width], cosine, sine, -1.0).astype(LOW),
            pair_grads[:, pair_width:].astype(LOW),
        ],
        axis=1,
    )
    grad_query, grad_key, grad_value = attn.scatter(normed_first, grad_projected, qkv_widths)
    grad_normed_first = attn.unspread(product_right(grad_projected, qkv_matrix))
    grad_input_norm, gain_first = rms_backward(inputs, rms_first, gains[0], grad_normed_first)
    grad_tokens = (grad_hidden + grad_input_norm).astype(LOW)
    gain_all = lax.psum(jnp.stack([gain_first, gain_second]), BOTH)
    gain_width = norm_gains.shape[1]
    gain_total = lax.dynamic_slice_in_dim(gain_all, lax.axis_index("dp") * gain_width, gain_width, 1)
    return (
        layer_out,
        grad_tokens,
        grad_query,
        grad_key,
        grad_value,
        grad_out,
        grad_gate,
        grad_up,
        grad_down,
        gain_total,
    )


def solution(mesh):
    placed = (
        P(("dp", "ctx"), None),
        P(("dp", "ctx")),
        P(("dp", "ctx")),
        P(("dp", "ctx")),
        P(("dp", "ctx")),
        P(("dp", "ctx")),
        P(("dp", "ctx")),
        P(("dp", "ctx")),
        P(None, "dp"),
        P(("dp", "ctx"), None),
    )
    dp_size, ctx_size = mesh.shape["dp"], mesh.shape["ctx"]
    return jax.shard_map(
        functools.partial(per_device, dp_size, ctx_size),
        mesh=mesh,
        in_specs=placed,
        out_specs=(
            P(("dp", "ctx"), None),
            P(("dp", "ctx"), None),
            P(("dp", "ctx")),
            P(("dp", "ctx")),
            P(("dp", "ctx")),
            P(("dp", "ctx")),
            P(("dp", "ctx")),
            P(("dp", "ctx")),
            P(("dp", "ctx")),
            P(None, "dp"),
        ),
        check_vma=False,
    )
```

time: 1170 us -> 599 us (0.51)
  waiting for transfers between devices: 628 us -> 169 us
  blocking collectives: 211 us -> 95.1 us
  other arithmetic: 123 us -> 55.7 us
  starting transfers between devices: 0.57 us -> 52.9 us
  local copies, waits for them, and re-layouts: 112 us -> 129 us
  between operations: 15.9 us -> 2.45 us
    unnamed x9 -> x0, waiting for transfers between devices: 534 us -> none
    ppermute x0 -> x46, waiting for transfers between devices: none -> 169 us  [swap(): lax.ppermute(values, axis, [(index, index ^ mask) for index in range(size)])]
    all_gather x2 -> x0, blocking collectives: 165 us -> none  [the longest x1 84.9 us: per_device(): lax.all_gather(w_value, ('dp', 'ctx'), axis=0, tiled=True)]
    all_gather x6 -> x0, waiting for transfers between devices: 94 us -> none  [the longest x1 47.1 us: per_device(): lax.all_gather(w_down, ('dp', 'ctx'), axis=0, tiled=True)]
    all_gather x4 -> x0, other arithmetic: 88.5 us -> none  [the longest x1 40.8 us: per_device(): lax.all_gather(w_query, ('dp', 'ctx'), axis=0, tiled=True)]
    psum x1, blocking collectives: 21.7 us -> 86 us  [per_device(): gain_all = lax.psum(jnp.stack([gain_first, gain_second]), BOTH)]
    ppermute x0 -> x46, starting transfers between devices: none -> 52.9 us  [swap(): lax.ppermute(values, axis, [(index, index ^ mask) for index in range(size)])]
    another operation x9 -> x1, local copies, waits for them, and re-layouts: 48.4 us -> 0.01 us  [per_device(): allowed = jnp.tile(places, groups)[:, None] >= key_places[None, :]]
  transfers between devices with their start and end apart: 8 -> 46, of which waited for: 3 -> 14; matrix products, arithmetic and copies ran while one was open for 20% -> 35% of each run, Pallas kernels for 0% -> 0%
where the time goes in v1:
time: 599 us; the launch traced here: 590 us
  waiting for transfers between devices  169 us (28%)
  local copies, waits for them, and re-layouts  129 us (22%)
  blocking collectives  95.1 us (16%)
  matrix products  85.3 us (14%)
  other arithmetic  55.7 us (9%)
  starting transfers between devices  52.9 us (9%)
    ppermute x46, waiting for transfers between devices, swap(): lax.ppermute(values, axis, [(index, index ^ mask) for index in range(size)])  169 us
    psum x1, blocking collectives, per_device(): gain_all = lax.psum(jnp.stack([gain_first, gain_second]), BOTH)  86 us
    ppermute x46, starting transfers between devices, swap(): lax.ppermute(values, axis, [(index, index ^ mask) for index in range(size)])  52.9 us
    concatenate x10, local copies, waits for them, and re-layouts, gather(): jnp.concatenate([block, swap(block, axis, self.sizes[axis], mask)], axis=0)  36.5 us
    dot_general x5, matrix products, batched(): return jnp.einsum(pattern, left, right, preferred_element_type=jnp.float32)  26 us
    unnamed x152, local copies, waits for them, and re-layouts  25.4 us
    concatenate x12, other arithmetic, gather(): jnp.concatenate([block, swap(block, axis, self.sizes[axis], mask)], axis=0)  18.4 us
    dot_general x7, matrix products, product(): return jnp.dot(left, right, preferred_element_type=jnp.float32)  16.8 us
  transfers between devices with their start and end apart: 46, of which 14 were waited for; matrix products, arithmetic and copies ran while one was open for 35% of the time, Pallas kernels for 0%

profile of v1, /device:TPU:0, one launch (start us, length us, event | category | flops | bytes accessed | tf_op | source)
XLA Modules:
  0.0 590.0 jit_solution(15589954015955978609)
XLA Ops:
  1.8 4.1 collective-permute-start.18
  18.8 9.1 %all-gather = bf16[8,120,2]{1,2,0:T(2,128)(2,1)S(1)} all-gather(bf16[1,120,2]{1,2,0:T(2,128)(2,1)S(1)} %bitcast.134), channel_id=1, replica_groups=mesh['dp'=8,'ctx'=4] {'dp'}, dimensions={0}, use_global_device_ids=true | all-gather | bytes 4320 | tf_op jit(solution)/shard_map/all_gather | solution.py:204
  37.1 12.0 %collective-permute-done.14 = bf16[64,5120]{1,0:T(8,128)(2,1)S(1)} collective-permute-done((bf16[64,5120]{1,0:T(8,128)(2,1)S(1)}, bf16[64,5120]{1,0:T(8,128)(2,1)S(1)}, u32[]{:S(2)}, u32[]{:S(2)}) %collective-permute-start.14) | collective-permute-done | bytes 655392 | tf_op jit(solution)/shard_map/ppermute | solution.py:40
  108.7 47.0 %collective-permute-done.20 = bf16[4,80,960]{2,1,0:T(8,128)(2,1)} collective-permute-done((bf16[4,80,960]{2,1,0:T(8,128)(2,1)}, bf16[4,80,960]{2,1,0:T(8,128)(2,1)}, u32[]{:S(2)}, u32[]{:S(2)}) %collective-permute-start.20) | collective-permute-done | bytes 614432 | tf_op jit(solution)/shard_map/ppermute | solution.py:40
  158.6 3.9 concatenate.117
  170.4 4.8 constant_dynamic-update-slice_fusion.5
  175.7 11.2 %collective-permute-done.21 = bf16[8,80,960]{2,1,0:T(8,128)(2,1)} collective-permute-done((bf16[8,80,960]{2,1,0:T(8,128)(2,1)}, bf16[8,80,960]{2,1,0:T(8,128)(2,1)}, u32[]{:S(2)}, u32[]{:S(2)}) %collective-permute-start.21) | collective-permute-done | bytes 1228832 | tf_op jit(solution)/shard_map/ppermute | solution.py:40
  190.1 6.8 %concatenate.118 = bf16[1024,1600]{0,1:T(8,128)(2,1)} concatenate(bf16[32,1600]{0,1:T(8,128)(2,1)S(1)} %copy-done.24, bf16[32,1600]{0,1:T(8,128)(2,1)S(1)} %copy-done.26, bf16[64,1600]{0,1:T(8,128)(2,1)S(1)} %copy-done.27, bf16[128,1600]{0,1:T(8,128)(2,1)} %copy.90, bf16[256,1600]{0,1:T(8,128)(2,1)} %collective-permute-done.3, bf16[512,1600]{0,1:T(8,128)(2,1)} %collective-permute-done.4), dimensions={0} | concatenate | bytes 6553600 | tf_op jit(solution)/shard_map/concatenate | solution.py:62
  201.5 5.4 collective-permute-start.6
  208.2 10.0 %collective-permute-done.5 = bf16[256,640]{0,1:T(8,128)(2,1)S(1)} collective-permute-done((bf16[256,640]{0,1:T(8,128)(2,1)S(1)}, bf16[256,640]{0,1:T(8,128)(2,1)S(1)}, u32[]{:S(2)}, u32[]{:S(2)}) %collective-permute-start.5) | collective-permute-done | bytes 327712 | tf_op jit(solution)/shard_map/ppermute | solution.py:40
  218.1 11.3 %collective-permute-done.6 = bf16[256,640]{0,1:T(8,128)(2,1)S(1)} collective-permute-done((bf16[256,640]{0,1:T(8,128)(2,1)S(1)}, bf16[256,640]{0,1:T(8,128)(2,1)S(1)}, u32[]{:S(2)}, u32[]{:S(2)}) %collective-permute-start.6) | collective-permute-done | bytes 327712 | tf_op jit(solution)/shard_map/ppermute | solution.py:40
  229.8 12.4 %fusion.94 = (f32[5,768]{1,0:T(8,128)S(1)}, f32[5,768,1024]{2,1,0:T(8,128)}) fusion(pred[768,1024]{1,0:T(8,128)(4,1)} %broadcast_compare_fusion, bf16[5,768,64]{1,2,0:T(8,128)(2,1)} %bitcast.109, bf16[5,1024,64]{1,2,0:T(8,128)(2,1)S(1)} %bitcast.105), kind=kOutput, calls=%fused_computation.240 | convolution fusion | flops 519046144 | bytes 17677312 | tf_op jit(solution)/shard_map/sub | solution.py:251
  242.3 9.1 %fusion.95 = (bf16[5,768,64]{1,2,0:T(8,128)(2,1)}, f32[5,768,64]{1,2,0:T(8,128)}) fusion(bf16[5,1024,64]{1,2,0:T(8,128)(2,1)S(1)} %bitcast.96, f32[5,768,1024]{2,1,0:T(8,128)} %get-tuple-element.78, f32[5,768]{1,0:T(8,128)S(1)} %broadcast_divide_fusion), kind=kOutput, calls=%fused_computation.241 | convolution fusion | flops 511426560 | bytes 17873920 | tf_op jit(solution)/shard_map/gqk,gkd->gqd/dot_general | solution.py:242
  259.7 5.9 gather_fusion
  265.6 5.4 broadcast_select_fusion.1
  271.0 5.2 constant_dynamic-update-slice_fusion.10
  276.3 6.1 %fusion.97 = f32[256,5120]{1,0:T(8,128)S(1)} fusion(bf16[256,1024]{1,0:T(8,128)(2,1)S(1)} %fusion.31, bf16[1024,5120]{1,0:T(8,128)(2,1)} %constant_dynamic-update-slice_fusion.10), kind=kOutput, calls=%fused_computation.243 | convolution fusion | flops 2684354560 | bytes 16252928 | tf_op jit(solution)/shard_map/dot_general | solution.py:20
  282.4 6.3 %multiply_convert_fusion.5 = (bf16[256,2560]{1,0:T(8,128)(2,1)S(1)}, bf16[256,2560]{1,0:T(8,128)(2,1)S(1)}, bf16[256,2560]{1,0:T(8,128)(2,1)}) fusion(f32[256,5120]{1,0:T(8,128)S(1)} %fusion.97, bf16[2560,960]{1,0:T(8,128)(2,1)} %bitcast.99, bf16[256,960]{0,1:T(8,128)(2,1)S(1)} %copy-done.29), kind=kOutput, calls=%fused_computation.40 | convolution fusion | flops 1268121600 | bytes 14581760 | tf_op jit(solution)/shard_map/dot_general | solution.py:30
  299.1 7.5 %multiply_convert_fusion = bf16[5,768,1024]{2,1,0:T(8,128)(2,1)S(1)} fusion(f32[5,768,1024]{2,1,0:T(8,128)} %get-tuple-element.78, bf16[5,768,64]{1,2,0:T(8,128)(2,1)S(1)} %reshape.383, bf16[5,1024,64]{1,2,0:T(8,128)(2,1)} %bitcast.97, f32[5,768]{1,0:T(8,128)S(1)} %multiply_reduce_fusion.1, f32[5,768]{1,0:T(8,128)S(1)} %broadcast_divide_fusion), kind=kOutput, calls=%fused_computation.3 | convolution fusion | flops 519045120 | bytes 24770560 | tf_op jit(solution)/shard_map/gqd,gkd->gqk/dot_general | solution.py:242
  306.6 5.0 convolution_multiply_fusion.1
  316.6 3.9 convolution_convert_fusion
  326.8 7.2 %collective-permute-start.23 = (bf16[256,640]{0,1:T(8,128)(2,1)}, bf16[256,640]{0,1:T(8,128)(2,1)}, u32[]{:S(2)}, u32[]{:S(2)}) collective-permute-start(bf16[256,640]{0,1:T(8,128)(2,1)} %bitcast.27), channel_id=1, source_target_pairs={{0,1},{1,0},{2,3},{3,2},{4,5},{5,4},{6,7},{7,6},{8,9},{9,8},{10,11... | collective-permute-start | bytes 983048 | tf_op jit(solution)/shard_map/ppermute | solution.py:40
  340.6 8.1 %copy.106 = bf16[2560,960]{1,0:T(8,128)(2,1)} copy(bf16[2560,960]{0,1:T(8,128)(2,1)} %convolution_convert_fusion.1) | data formatting | bytes 9830400 | tf_op jit(solution)/shard_map/convert_element_type | solution.py:268
  348.7 5.8 gather_fusion.1
  376.9 11.5 %collective-permute-done.32 = bf16[256,960]{0,1:T(8,128)(2,1)S(1)} collective-permute-done((bf16[256,960]{0,1:T(8,128)(2,1)S(1)}, bf16[256,960]{0,1:T(8,128)(2,1)S(1)}, u32[]{:S(2)}, u32[]{:S(2)}) %collective-permute-start.32) | collective-permute-done | bytes 491552 | tf_op jit(solution)/shard_map/ppermute | solution.py:40
  389.7 4.0 add_convert_fusion
  400.4 86.0 %psum.7 = f32[2,960]{1,0:T(2,128)S(1)} all-reduce(f32[2,960]{1,0:T(2,128)S(1)} %pad_maximum_fusion.25), channel_id=1, replica_groups=mesh['dp'=8,'ctx'=4] {'dp','ctx'}, use_global_device_ids=true, to_apply=%region_10.12 | all-reduce | flops 1920 | bytes 15360 | tf_op jit(solution)/shard_map/psum | solution.py:313
  508.1 20.1 %collective-permute-done.42 = bf16[8,80,960]{2,1,0:T(8,128)(2,1)S(1)} collective-permute-done((bf16[8,80,960]{2,1,0:T(8,128)(2,1)S(1)}, bf16[8,80,960]{2,1,0:T(8,128)(2,1)S(1)}, u32[]{:S(2)}, u32[]{:S(2)}) %collective-permute-start.42) | collective-permute-done | bytes 1228832 | tf_op jit(solution)/shard_map/ppermute | solution.py:40
  536.9 5.0 collective-permute-done.43
  544.5 9.0 %collective-permute-done.38 = bf16[128,5120]{1,0:T(8,128)(2,1)} collective-permute-done((bf16[128,5120]{1,0:T(8,128)(2,1)}, bf16[128,5120]{1,0:T(8,128)(2,1)}, u32[]{:S(2)}, u32[]{:S(2)}) %collective-permute-start.38) | collective-permute-done | bytes 1310752 | tf_op jit(solution)/shard_map/ppermute | solution.py:40
  558.3 14.2 %collective-permute-done.39 = bf16[64,5120]{1,0:T(8,128)(2,1)S(1)} collective-permute-done((bf16[64,5120]{1,0:T(8,128)(2,1)S(1)}, bf16[64,5120]{1,0:T(8,128)(2,1)S(1)}, u32[]{:S(2)}, u32[]{:S(2)}) %collective-permute-start.39) | collective-permute-done | bytes 655392 | tf_op jit(solution)/shard_map/ppermute | solution.py:40
  576.7 11.2 %collective-permute-done.40 = bf16[32,5120]{1,0:T(8,128)(2,1)S(1)} collective-permute-done((bf16[32,5120]{1,0:T(8,128)(2,1)S(1)}, bf16[32,5120]{1,0:T(8,128)(2,1)S(1)}, u32[]{:S(2)}, u32[]{:S(2)}) %collective-permute-start.40) | collective-permute-done | bytes 327712 | tf_op jit(solution)/shard_map/ppermute | solution.py:40
  (405 shorter events, 212.8 us)
Async XLA Ops:
  1.8 64.0 %collective-permute-start.18 = (bf16[1,80,960]{2,1,0:T(8,128)(2,1)S(1)}, bf16[1,80,960]{2,1,0:T(8,128)(2,1)S(1)}, u32[]{:S(2)}, u32[]{:S(2)}) collective-permute-start(bf16[1,80,960]{2,1,0:T(8,128)(2,1)S(1)} %reshape.380), channel_id=1, source_target_pairs={{0,2},{1,3},{2,0},{3,1},{4,6},{5,7},{6,4},{7,5},{8,10},{9,11},{10,... | collective-permute-start | bytes 460808 | tf_op jit(solution)/shard_map/ppermute | solution.py:40
  9.1 23.1 %collective-permute-start.13 = (bf16[32,5120]{1,0:T(8,128)(2,1)S(1)}, bf16[32,5120]{1,0:T(8,128)(2,1)S(1)}, u32[]{:S(2)}, u32[]{:S(2)}) collective-permute-start(bf16[32,5120]{1,0:T(8,128)(2,1)S(1)} %get-tuple-element.55), channel_id=1, source_target_pairs={{0,2},{1,3},{2,0},{3,1},{4,6},{5,7},{6,4},{7,5},{8,10},{9,11},{10,... | collective-permute-start | bytes 983048 | tf_op jit(solution)/shard_map/ppermute | solution.py:40
  11.8 48.6 %collective-permute-start = (bf16[32,1600]{1,0:T(8,128)(2,1)S(1)}, bf16[32,1600]{1,0:T(8,128)(2,1)}, u32[]{:S(2)}, u32[]{:S(2)}) collective-permute-start(bf16[32,1600]{1,0:T(8,128)(2,1)S(1)} %pad.12), channel_id=1, source_target_pairs={{0,2},{1,3},{2,0},{3,1},{4,6},{5,7},{6,4},{7,5},{8,10},{9,11},{10,... | collective-permute-start | bytes 307208 | tf_op jit(solution)/shard_map/ppermute | solution.py:40
  15.5 40.1 %collective-permute-start.8 = (bf16[32,960]{1,0:T(8,128)(2,1)}, bf16[32,960]{1,0:T(8,128)(2,1)}, u32[]{:S(2)}, u32[]{:S(2)}) collective-permute-start(bf16[32,960]{1,0:T(8,128)(2,1)} %get-tuple-element.63), channel_id=1, source_target_pairs={{0,2},{1,3},{2,0},{3,1},{4,6},{5,7},{6,4},{7,5},{8,10},{9,11},{10,... | collective-permute-start | bytes 184328 | tf_op jit(solution)/shard_map/ppermute | solution.py:40
  50.2 30.1 %collective-permute-start.15 = (bf16[128,5120]{1,0:T(8,128)(2,1)}, bf16[128,5120]{1,0:T(8,128)(2,1)S(1)}, u32[]{:S(2)}, u32[]{:S(2)}) collective-permute-start(bf16[128,5120]{1,0:T(8,128)(2,1)} %pad_maximum_fusion.3), channel_id=1, source_target_pairs={{0,16},{4,20},{8,24},{12,28},{16,0},{20,4},{24,8},{28,12},{1,17},{... | collective-permute-start | bytes 3932168 | tf_op jit(solution)/shard_map/ppermute | solution.py:40
  66.6 24.4 %collective-permute-start.19 = (bf16[2,80,960]{2,1,0:T(8,128)(2,1)}, bf16[2,80,960]{2,1,0:T(8,128)(2,1)}, u32[]{:S(2)}, u32[]{:S(2)}) collective-permute-start(bf16[2,80,960]{2,1,0:T(8,128)(2,1)} %pad_maximum_fusion.19), channel_id=1, source_target_pairs={{0,1},{1,0},{2,3},{3,2},{4,5},{5,4},{6,7},{7,6},{8,9},{9,8},{10,11... | collective-permute-start | bytes 921608 | tf_op jit(solution)/shard_map/ppermute | solution.py:40
  75.7 17.8 %collective-permute-start.2 = (bf16[128,1600]{1,0:T(8,128)(2,1)}, bf16[128,1600]{1,0:T(8,128)(2,1)}, u32[]{:S(2)}, u32[]{:S(2)}) collective-permute-start(bf16[128,1600]{1,0:T(8,128)(2,1)} %pad_maximum_fusion.17), channel_id=1, source_target_pairs={{0,8},{4,12},{8,0},{12,4},{16,24},{20,28},{24,16},{28,20},{1,9},{5... | collective-permute-start | bytes 1228808 | tf_op jit(solution)/shard_map/ppermute | solution.py:40
  82.0 88.4 %collective-permute-start.16 = (bf16[256,5120]{1,0:T(8,128)(2,1)}, bf16[256,5120]{1,0:T(8,128)(2,1)}, u32[]{:S(2)}, u32[]{:S(2)}) collective-permute-start(bf16[256,5120]{1,0:T(8,128)(2,1)} %pad_maximum_fusion), channel_id=1, source_target_pairs={{0,8},{4,12},{8,0},{12,4},{16,24},{20,28},{24,16},{28,20},{1,9},{5... | collective-permute-start | bytes 7864328 | tf_op jit(solution)/shard_map/ppermute | solution.py:40
  92.9 62.9 %collective-permute-start.20 = (bf16[4,80,960]{2,1,0:T(8,128)(2,1)}, bf16[4,80,960]{2,1,0:T(8,128)(2,1)}, u32[]{:S(2)}, u32[]{:S(2)}) collective-permute-start(bf16[4,80,960]{2,1,0:T(8,128)(2,1)} %pad_maximum_fusion.13), channel_id=1, source_target_pairs={{0,8},{4,12},{8,0},{12,4},{16,24},{20,28},{24,16},{28,20},{1,9},{5... | collective-permute-start | bytes 1843208 | tf_op jit(solution)/shard_map/ppermute | solution.py:40
  97.7 60.9 %collective-permute-start.3 = (bf16[256,1600]{0,1:T(8,128)(2,1)}, bf16[256,1600]{0,1:T(8,128)(2,1)}, u32[]{:S(2)}, u32[]{:S(2)}) collective-permute-start(bf16[256,1600]{0,1:T(8,128)(2,1)} %copy.82), channel_id=1, source_target_pairs={{0,16},{4,20},{8,24},{12,28},{16,0},{20,4},{24,8},{28,12},{1,17},{... | collective-permute-start | bytes 2457608 | tf_op jit(solution)/shard_map/ppermute | solution.py:40
  101.6 63.2 %collective-permute-start.12 = (bf16[512,960]{0,1:T(8,128)(2,1)}, bf16[512,960]{0,1:T(8,128)(2,1)}, u32[]{:S(2)}, u32[]{:S(2)}) collective-permute-start(bf16[512,960]{0,1:T(8,128)(2,1)} %copy.93), channel_id=1, source_target_pairs={{0,4},{4,0},{8,12},{12,8},{16,20},{20,16},{24,28},{28,24},{1,5},{5... | collective-permute-start | bytes 2949128 | tf_op jit(solution)/shard_map/ppermute | solution.py:40
  158.1 28.9 %collective-permute-start.21 = (bf16[8,80,960]{2,1,0:T(8,128)(2,1)}, bf16[8,80,960]{2,1,0:T(8,128)(2,1)}, u32[]{:S(2)}, u32[]{:S(2)}) collective-permute-start(bf16[8,80,960]{2,1,0:T(8,128)(2,1)} %pad_maximum_fusion.4), channel_id=1, source_target_pairs={{0,16},{4,20},{8,24},{12,28},{16,0},{20,4},{24,8},{28,12},{1,17},{... | collective-permute-start | bytes 3686408 | tf_op jit(solution)/shard_map/ppermute | solution.py:40
  162.5 27.6 %collective-permute-start.4 = (bf16[512,1600]{0,1:T(8,128)(2,1)}, bf16[512,1600]{0,1:T(8,128)(2,1)}, u32[]{:S(2)}, u32[]{:S(2)}) collective-permute-start(bf16[512,1600]{0,1:T(8,128)(2,1)} %concatenate.117), channel_id=1, source_target_pairs={{0,4},{4,0},{8,12},{12,8},{16,20},{20,16},{24,28},{28,24},{1,5},{5... | collective-permute-start | bytes 4915208 | tf_op jit(solution)/shard_map/ppermute | solution.py:40
  175.2 95.8 %collective-permute-start.17 = (bf16[512,5120]{1,0:T(8,128)(2,1)}, bf16[512,5120]{1,0:T(8,128)(2,1)}, u32[]{:S(2)}, u32[]{:S(2)}) collective-permute-start(bf16[512,5120]{1,0:T(8,128)(2,1)} %get-tuple-element.22), channel_id=1, source_target_pairs={{0,4},{4,0},{8,12},{12,8},{16,20},{20,16},{24,28},{28,24},{1,5},{5... | collective-permute-start | bytes 15728648 | tf_op jit(solution)/shard_map/ppermute | solution.py:40
  190.1 65.8 %collective-permute-start.22 = (bf16[16,80,960]{2,1,0:T(8,128)(2,1)}, bf16[16,80,960]{2,1,0:T(8,128)(2,1)}, u32[]{:S(2)}, u32[]{:S(2)}) collective-permute-start(bf16[16,80,960]{2,1,0:T(8,128)(2,1)} %get-tuple-element.27), channel_id=1, source_target_pairs={{0,4},{4,0},{8,12},{12,8},{16,20},{20,16},{24,28},{28,24},{1,5},{5... | collective-permute-start | bytes 7372808 | tf_op jit(solution)/shard_map/ppermute | solution.py:40
  201.5 28.0 %collective-permute-start.6 = (bf16[256,640]{0,1:T(8,128)(2,1)S(1)}, bf16[256,640]{0,1:T(8,128)(2,1)S(1)}, u32[]{:S(2)}, u32[]{:S(2)}) collective-permute-start(bf16[256,640]{0,1:T(8,128)(2,1)S(1)} %pad_maximum_fusion.18), channel_id=1, source_target_pairs={{0,2},{1,3},{2,0},{3,1},{4,6},{5,7},{6,4},{7,5},{8,10},{9,11},{10,... | collective-permute-start | bytes 983048 | tf_op jit(solution)/shard_map/ppermute | solution.py:40
  206.9 22.6 %collective-permute-start.7 = (bf16[256,640]{0,1:T(8,128)(2,1)S(1)}, bf16[256,640]{0,1:T(8,128)(2,1)S(1)}, u32[]{:S(2)}, u32[]{:S(2)}) collective-permute-start(bf16[256,640]{0,1:T(8,128)(2,1)S(1)} %pad_maximum_fusion.18), channel_id=1, source_target_pairs={{0,3},{1,2},{2,1},{3,0},{4,7},{5,6},{6,5},{7,4},{8,11},{9,10},{10,... | collective-permute-start | bytes 983048 | tf_op jit(solution)/shard_map/ppermute | solution.py:40
  320.5 69.1 %collective-permute-start.36 = (bf16[512,5120]{1,0:T(8,128)(2,1)}, bf16[512,5120]{1,0:T(8,128)(2,1)}, u32[]{:S(2)}, u32[]{:S(2)}) collective-permute-start(bf16[512,5120]{1,0:T(8,128)(2,1)} %convolution_convert_fusion), channel_id=1, source_target_pairs={{0,4},{4,0},{8,12},{12,8},{16,20},{20,16},{24,28},{28,24},{1,5},{5... | collective-permute-start | bytes 15728648 | tf_op jit(solution)/shard_map/ppermute | solution.py:40
  326.8 40.7 %collective-permute-start.23 = (bf16[256,640]{0,1:T(8,128)(2,1)}, bf16[256,640]{0,1:T(8,128)(2,1)}, u32[]{:S(2)}, u32[]{:S(2)}) collective-permute-start(bf16[256,640]{0,1:T(8,128)(2,1)} %bitcast.27), channel_id=1, source_target_pairs={{0,1},{1,0},{2,3},{3,2},{4,5},{5,4},{6,7},{7,6},{8,9},{9,8},{10,11... | collective-permute-start | bytes 983048 | tf_op jit(solution)/shard_map/ppermute | solution.py:40
  334.0 33.6 %collective-permute-start.24 = (bf16[256,640]{0,1:T(8,128)(2,1)}, bf16[256,640]{0,1:T(8,128)(2,1)}, u32[]{:S(2)}, u32[]{:S(2)}) collective-permute-start(bf16[256,640]{0,1:T(8,128)(2,1)} %bitcast.28), channel_id=1, source_target_pairs={{0,2},{1,3},{2,0},{3,1},{4,6},{5,7},{6,4},{7,5},{8,10},{9,11},{10,... | collective-permute-start | bytes 983048 | tf_op jit(solution)/shard_map/ppermute | solution.py:40
  335.5 32.2 %collective-permute-start.25 = (bf16[256,640]{0,1:T(8,128)(2,1)}, bf16[256,640]{0,1:T(8,128)(2,1)}, u32[]{:S(2)}, u32[]{:S(2)}) collective-permute-start(bf16[256,640]{0,1:T(8,128)(2,1)} %bitcast.29), channel_id=1, source_target_pairs={{0,3},{1,2},{2,1},{3,0},{4,7},{5,6},{6,5},{7,4},{8,11},{9,10},{10,... | collective-permute-start | bytes 983048 | tf_op jit(solution)/shard_map/ppermute | solution.py:40
  359.6 132.9 %collective-permute-start.41 = (bf16[16,80,960]{2,1,0:T(8,128)(2,1)}, bf16[16,80,960]{2,1,0:T(8,128)(2,1)}, u32[]{:S(2)}, u32[]{:S(2)}) collective-permute-start(bf16[16,80,960]{2,1,0:T(8,128)(2,1)} %slice.359), channel_id=1, source_target_pairs={{0,4},{4,0},{8,12},{12,8},{16,20},{20,16},{24,28},{28,24},{1,5},{5... | collective-permute-start | bytes 7372808 | tf_op jit(solution)/shard_map/ppermute | solution.py:40
  370.2 26.8 %collective-permute-start.26 = (bf16[512,1600]{0,1:T(8,128)(2,1)S(1)}, bf16[512,1600]{0,1:T(8,128)(2,1)S(1)}, u32[]{:S(2)}, u32[]{:S(2)}) collective-permute-start(bf16[512,1600]{0,1:T(8,128)(2,1)S(1)} %convolution_convert_fusion.2), channel_id=1, source_target_pairs={{0,4},{4,0},{8,12},{12,8},{16,20},{20,16},{24,28},{28,24},{1,5},{5... | collective-permute-start | bytes 4915208 | tf_op jit(solution)/shard_map/ppermute | solution.py:40
  396.1 106.4 %collective-permute-start.37 = (bf16[256,5120]{1,0:T(8,128)(2,1)S(1)}, bf16[256,5120]{1,0:T(8,128)(2,1)}, u32[]{:S(2)}, u32[]{:S(2)}) collective-permute-start(bf16[256,5120]{1,0:T(8,128)(2,1)S(1)} %slice.349), channel_id=1, source_target_pairs={{0,8},{4,12},{8,0},{12,4},{16,24},{20,28},{24,16},{28,20},{1,9},{5... | collective-permute-start | bytes 7864328 | tf_op jit(solution)/shard_map/ppermute | solution.py:40
  398.7 89.8 %collective-permute-start.27 = (bf16[256,1600]{0,1:T(8,128)(2,1)}, bf16[256,1600]{0,1:T(8,128)(2,1)}, u32[]{:S(2)}, u32[]{:S(2)}) collective-permute-start(bf16[256,1600]{0,1:T(8,128)(2,1)} %slice.324), channel_id=1, source_target_pairs={{0,16},{4,20},{8,24},{12,28},{16,0},{20,4},{24,8},{28,12},{1,17},{... | collective-permute-start | bytes 2457608 | tf_op jit(solution)/shard_map/ppermute | solution.py:40
  399.4 87.6 %collective-permute-start.34 = (bf16[64,960]{0,1:T(8,128)(2,1)S(1)}, bf16[64,960]{0,1:T(8,128)(2,1)S(1)}, u32[]{:S(2)}, u32[]{:S(2)}) collective-permute-start(bf16[64,960]{0,1:T(8,128)(2,1)S(1)} %slice.341), channel_id=1, source_target_pairs={{0,1},{1,0},{2,3},{3,2},{4,5},{5,4},{6,7},{7,6},{8,9},{9,8},{10,11... | collective-permute-start | bytes 368648 | tf_op jit(solution)/shard_map/ppermute | solution.py:40
  487.3 44.0 %collective-permute-start.35 = (bf16[32,960]{0,1:T(8,128)(2,1)S(1)}, bf16[32,960]{0,1:T(8,128)(2,1)S(1)}, u32[]{:S(2)}, u32[]{:S(2)}) collective-permute-start(bf16[32,960]{0,1:T(8,128)(2,1)S(1)} %get-tuple-element.57), channel_id=1, source_target_pairs={{0,2},{1,3},{2,0},{3,1},{4,6},{5,7},{6,4},{7,5},{8,10},{9,11},{10,... | collective-permute-start | bytes 184328 | tf_op jit(solution)/shard_map/ppermute | solution.py:40
  496.5 31.8 %collective-permute-start.42 = (bf16[8,80,960]{2,1,0:T(8,128)(2,1)S(1)}, bf16[8,80,960]{2,1,0:T(8,128)(2,1)S(1)}, u32[]{:S(2)}, u32[]{:S(2)}) collective-permute-start(bf16[8,80,960]{2,1,0:T(8,128)(2,1)S(1)} %slice.361), channel_id=1, source_target_pairs={{0,16},{4,20},{8,24},{12,28},{16,0},{20,4},{24,8},{28,12},{1,17},{... | collective-permute-start | bytes 3686408 | tf_op jit(solution)/shard_map/ppermute | solution.py:40
  501.6 32.3 %collective-permute-start.29 = (bf16[64,1600]{0,1:T(8,128)(2,1)}, bf16[64,1600]{0,1:T(8,128)(2,1)}, u32[]{:S(2)}, u32[]{:S(2)}) collective-permute-start(bf16[64,1600]{0,1:T(8,128)(2,1)} %slice.328), channel_id=1, source_target_pairs={{0,1},{1,0},{2,3},{3,2},{4,5},{5,4},{6,7},{7,6},{8,9},{9,8},{10,11... | collective-permute-start | bytes 614408 | tf_op jit(solution)/shard_map/ppermute | solution.py:40
  506.4 47.1 %collective-permute-start.38 = (bf16[128,5120]{1,0:T(8,128)(2,1)}, bf16[128,5120]{1,0:T(8,128)(2,1)}, u32[]{:S(2)}, u32[]{:S(2)}) collective-permute-start(bf16[128,5120]{1,0:T(8,128)(2,1)} %slice.351), channel_id=1, source_target_pairs={{0,16},{4,20},{8,24},{12,28},{16,0},{20,4},{24,8},{28,12},{1,17},{... | collective-permute-start | bytes 3932168 | tf_op jit(solution)/shard_map/ppermute | solution.py:40
  535.2 21.0 %collective-permute-start.30 = (bf16[32,1600]{0,1:T(8,128)(2,1)S(1)}, bf16[32,1600]{0,1:T(8,128)(2,1)S(1)}, u32[]{:S(2)}, u32[]{:S(2)}) collective-permute-start(bf16[32,1600]{0,1:T(8,128)(2,1)S(1)} %slice.330), channel_id=1, source_target_pairs={{0,2},{1,3},{2,0},{3,1},{4,6},{5,7},{6,4},{7,5},{8,10},{9,11},{10,... | collective-permute-start | bytes 307208 | tf_op jit(solution)/shard_map/ppermute | solution.py:40
  556.3 19.4 %collective-permute-start.45 = (bf16[1,80,960]{2,1,0:T(8,128)(2,1)S(1)}, bf16[1,80,960]{2,1,0:T(8,128)(2,1)S(1)}, u32[]{:S(2)}, u32[]{:S(2)}) collective-permute-start(bf16[1,80,960]{2,1,0:T(8,128)(2,1)S(1)} %slice.367), channel_id=1, source_target_pairs={{0,2},{1,3},{2,0},{3,1},{4,6},{5,7},{6,4},{7,5},{8,10},{9,11},{10,... | collective-permute-start | bytes 460808 | tf_op jit(solution)/shard_map/ppermute | solution.py:40
  (85 other events, 1044.1 us)

commit v2 on v1

--- a/solution.py
+++ b/solution.py
@@ -45,12 +45,10 @@
 
 
 class Exchange:
-    def __init__(self, dp_size, ctx_size, dp_bits):
-        stages = [("ctx", mask) for mask in reversed(bits_of(ctx_size))]
-        stages += [("dp", mask) for mask in dp_bits] + [("dp", 1)]
+    def __init__(self, dp_size, ctx_size, stages):
         self.stages = stages
         self.sizes = {"dp": dp_size, "ctx": ctx_size}
-        self.count = dp_size * ctx_size
+        self.count = 1 << len(stages)
         slots = jnp.arange(self.count, dtype=jnp.int32)
         place = {"dp": lax.axis_index("dp"), "ctx": lax.axis_index("ctx")}
         for index, (axis, mask) in enumerate(stages):
@@ -79,6 +77,17 @@
         return (feature[:, None] == source[None, :]).astype(LOW)
 
 
+def sum_gains(values, dp_size, ctx_size):
+    width = values.shape[1] // dp_size
+    slots = lax.axis_index("dp") ^ jnp.arange(dp_size, dtype=jnp.int32)
+    blocks = jnp.take(values.reshape(2, dp_size, width).transpose(1, 0, 2), slots, axis=0)
+    for mask in reversed(bits_of(dp_size)):
+        blocks = blocks[:mask] + swap(blocks[mask:], "dp", dp_size, mask)
+    for mask in bits_of(ctx_size):
+        blocks = blocks + swap(blocks, "ctx", ctx_size, mask)
+    return blocks[0]
+
+
 class RowWeights:
     def __init__(self, exchange, rows):
         self.exchange, self.rows = exchange, rows
@@ -102,9 +111,88 @@
     def scatter(self, left, right, widths):
         half = left.shape[1] // 2
         send = product_left(left[:, half:], right).astype(LOW)
+        right, send = lax.optimization_barrier((right, send))
         total = self.exchange.scatter(product_left(left[:, :half], right), send)[: self.rows]
         cuts = [sum(widths[:index]) for index in range(len(widths) + 1)]
-        return [total[:, low:high].reshape(-1) for low, high in zip(cuts[:-1], cuts[1:])]
+        return right, [total[:, low:high].reshape(-1) for low, high in zip(cuts[:-1], cuts[1:])]
+
+
+class SplitFeed:
+    def __init__(self, dp_size, ctx_size, rows, last_rows, up_bits, down_bits):
+        near = [("ctx", mask) for mask in reversed(bits_of(ctx_size))]
+        core = [("dp", 1)]
+        self.outer = Exchange(dp_size, ctx_size, near + [("dp", mask) for mask in up_bits])
+        self.down = Exchange(dp_size, ctx_size, near + [("dp", mask) for mask in down_bits])
+        order = Exchange(dp_size, ctx_size, core + self.outer.stages)
+        self.weights = RowWeights(order, rows)
+        self.rows, self.last_rows, self.dp_size = rows, last_rows, dp_size
+        self.core = lax.axis_index("dp") % 2
+        self.run = ctx_size * last_rows
+        self.ranks = self.down.shard // ctx_size // 2 * ctx_size + self.down.shard % ctx_size
+
+    def partner(self, values):
+        return swap(values, "dp", self.dp_size, 1)
+
+    def gather(self, gate, up, down):
+        block = jnp.stack([flat.reshape(self.rows, -1, 2, self.run) for flat in (gate, up)], axis=1)
+        padding = ((0, self.weights.padded - self.rows), (0, 0))
+        first, second = (
+            jnp.pad(block[:, :, :, core].reshape(self.rows, -1), padding) for core in range(2)
+        )
+        keep = jnp.where(self.core == 0, first, second)
+        send = jnp.where(self.core == 0, second, first)
+        matrix = self.outer.gather(jnp.concatenate([keep, self.partner(send)], axis=0))
+        slots = self.down.gather(down.reshape(1, self.last_rows, D))
+        return matrix, jnp.take(slots, jnp.argsort(self.ranks), axis=0).reshape(-1, D)
+
+    def both(self, values):
+        return jnp.concatenate([values, self.partner(values)], axis=0)
+
+    def own(self, values):
+        half = values.shape[0] // 2
+        return values[:half] + self.partner(values[half:].astype(LOW)).astype(jnp.float32)
+
+    def scatter_down(self, active, cotangent):
+        blocks = product_left(active, cotangent).astype(LOW).reshape(-1, self.last_rows, D)
+        blocks = jnp.take(blocks, self.ranks, axis=0)
+        cotangent, blocks = lax.optimization_barrier((cotangent, blocks))
+        half = blocks.shape[0] // 2
+        return cotangent, self.down.scatter(blocks[:half], blocks[half:]).reshape(-1)
+
+    def scatter(self, left, right):
+        half = left.shape[1] // 2
+        send = product_left(left[:, half:], right).astype(LOW)
+        right, send = lax.optimization_barrier((right, send))
+        total = self.outer.scatter(product_left(left[:, :half], right), send)
+        padded = self.weights.padded
+        keep = total[:padded]
+        got = self.partner(total[padded:].astype(LOW)).astype(jnp.float32)
+        first = jnp.where(self.core == 0, keep, got)[: self.rows]
+        second = jnp.where(self.core == 0, got, keep)[: self.rows]
+        shape = (self.rows, 2, -1, self.run)
+        block = jnp.stack([first.reshape(shape), second.reshape(shape)], axis=3)
+        return right, (block[:, 0].reshape(-1), block[:, 1].reshape(-1))
+
+
+class FlatFeed:
+    def __init__(self):
+        self.weights = FlatWeights()
+
+    def gather(self, gate, up, down):
+        return self.weights.gather((gate, up), (FF, FF)), self.weights.gather((down,), (D,))
+
+    def both(self, values):
+        return values
+
+    def own(self, values):
+        return values
+
+    def scatter_down(self, active, cotangent):
+        cotangent, (grad,) = self.weights.scatter(active, cotangent, (D,))
+        return cotangent, grad
+
+    def scatter(self, left, right):
+        return self.weights.scatter(left, right, (FF, FF))
 
 
 class FlatWeights:
@@ -125,7 +213,7 @@
 
     def scatter(self, left, right, widths):
         cuts = [sum(widths[:index]) for index in range(len(widths) + 1)]
-        return [
+        return right, [
             lax.psum_scatter(
                 product_left(left, right[:, low:high]).astype(LOW).reshape(-1),
                 BOTH,
@@ -193,23 +281,19 @@
     qkv_widths = (query_width, pair_width, pair_width)
     if by_rows:
         dp_bits = bits_of(dp_size)[1:]
-        exchange_up = Exchange(dp_size, ctx_size, dp_bits)
-        exchange_down = Exchange(dp_size, ctx_size, dp_bits[::-1])
-        attn = RowWeights(exchange_up, D // devices)
-        feed = RowWeights(exchange_down, D // devices)
-        last_rows = FF // devices
+        rows = D // devices
+        stages = [("ctx", mask) for mask in reversed(bits_of(ctx_size))]
+        stages += [("dp", mask) for mask in dp_bits] + [("dp", 1)]
+        attn = RowWeights(Exchange(dp_size, ctx_size, stages), rows)
+        feed = SplitFeed(dp_size, ctx_size, rows, FF // devices, dp_bits[::-1], dp_bits)
     else:
-        attn = feed = FlatWeights()
+        attn, feed = FlatWeights(), FlatFeed()
 
     gains = lax.all_gather(norm_gains, "dp", axis=1, tiled=True).astype(jnp.float32)
     qkv_matrix = attn.gather((w_query, w_key, w_value), qkv_widths)
     out_matrix = attn.gather((w_out,), (D,))
-    feed_matrix = feed.gather((w_gate, w_up), (FF, FF))
-    if by_rows:
-        slots = exchange_up.gather(w_down.reshape(1, last_rows, D))
-        down_matrix = jnp.take(slots, jnp.argsort(exchange_up.shard), axis=0).reshape(FF, D)
-    else:
-        down_matrix = feed.gather((w_down,), (D,))
+    feed_matrix, down_matrix = feed.gather(w_gate, w_up, w_down)
+    all_cotangents = feed.both(cotangent)
 
     ctx_place = lax.axis_index("ctx")
     inner = jnp.arange(local_rows, dtype=jnp.int32)
@@ -256,34 +340,30 @@
 
     hidden = inputs + product(mixed_low, out_matrix)
     scaled_second, rms_second = rms_forward(hidden, gains[1])
-    normed_second = feed.spread(scaled_second.astype(LOW))
+    normed_second = feed.weights.spread(feed.both(scaled_second.astype(LOW)))
     gate_up = product(normed_second, feed_matrix)
-    gate_values, up_values = gate_up[:, :FF], gate_up[:, FF:]
+    units = gate_up.shape[1] // 2
+    gate_values, up_values = gate_up[:, :units], gate_up[:, units:]
     sigmoid_gate = jax.nn.sigmoid(gate_values)
     silu_gate = gate_values * sigmoid_gate
     active = (silu_gate * up_values).astype(LOW)
-    layer_out = (hidden + product(active, down_matrix)).astype(LOW)
-
-    if by_rows:
-        blocks = product_left(active, cotangent).astype(LOW).reshape(devices, last_rows, D)
-        blocks = jnp.take(blocks, exchange_up.shard, axis=0)
-        grad_down = exchange_up.scatter(blocks[: devices // 2], blocks[devices // 2 :]).reshape(-1)
-    else:
-        (grad_down,) = feed.scatter(active, cotangent, (D,))
+    layer_out = (hidden + feed.own(product(active, down_matrix))).astype(LOW)
+
+    all_cotangents, grad_down = feed.scatter_down(active, all_cotangents)
     grad_layer = cotangent.astype(jnp.float32)
-    grad_active = product_right(cotangent, down_matrix)
+    grad_active = product_right(all_cotangents, down_matrix)
     grad_gate_values = grad_active * up_values * (
         sigmoid_gate * (1.0 + gate_values * (1.0 - sigmoid_gate))
     )
     grad_feed = jnp.concatenate(
         [grad_gate_values.astype(LOW), (grad_active * silu_gate).astype(LOW)], axis=1
     )
-    grad_gate, grad_up = feed.scatter(normed_second, grad_feed, (FF, FF))
-    grad_normed_second = feed.unspread(product_right(grad_feed, feed_matrix))
+    grad_feed, (grad_gate, grad_up) = feed.scatter(normed_second, grad_feed)
+    grad_normed_second = feed.own(feed.weights.unspread(product_right(grad_feed, feed_matrix)))
     grad_hidden_norm, gain_second = rms_backward(hidden, rms_second, gains[1], grad_normed_second)
     grad_hidden = grad_layer + grad_hidden_norm
     grad_attn = grad_hidden.astype(LOW)
-    (grad_out,) = attn.scatter(mixed_low, grad_attn, (D,))
+    grad_attn, (grad_out,) = attn.scatter(mixed_low, grad_attn, (D,))
     grad_mixed = attn.unspread(product_right(grad_attn, out_matrix)).astype(LOW)
 
     grad_heads = by_head(grad_mixed)
@@ -306,13 +386,13 @@
         ],
         axis=1,
     )
-    grad_query, grad_key, grad_value = attn.scatter(normed_first, grad_projected, qkv_widths)
+    grad_projected, (grad_query, grad_key, grad_value) = attn.scatter(
+        normed_first, grad_projected, qkv_widths
+    )
     grad_normed_first = attn.unspread(product_right(grad_projected, qkv_matrix))
     grad_input_norm, gain_first = rms_backward(inputs, rms_first, gains[0], grad_normed_first)
     grad_tokens = (grad_hidden + grad_input_norm).astype(LOW)
-    gain_all = lax.psum(jnp.stack([gain_first, gain_second]), BOTH)
-    gain_width = norm_gains.shape[1]
-    gain_total = lax.dynamic_slice_in_dim(gain_all, lax.axis_index("dp") * gain_width, gain_width, 1)
+    gain_total = sum_gains(jnp.stack([gain_first, gain_second]), dp_size, ctx_size)
     return (
         layer_out,
         grad_tokens,

time: 599 us -> 518 us (0.86)
  blocking collectives: 95.1 us -> 8.74 us
  waiting for transfers between devices: 169 us -> 216 us
  local copies, waits for them, and re-layouts: 129 us -> 102 us
  other arithmetic: 55.7 us -> 39.6 us
    psum x1 -> x0, blocking collectives: 86 us -> none  [per_device(): gain_all = lax.psum(jnp.stack([gain_first, gain_second]), BOTH)]
    ppermute x46 -> x53, waiting for transfers between devices: 169 us -> 216 us  [swap(): lax.ppermute(values, axis, [(index, index ^ mask) for index in range(size)])]
    convert_element_type x13 -> x11, other arithmetic: 13.5 us -> 4.49 us  [scatter(): total = total.astype(LOW)]
    concatenate x10 -> x9, local copies, waits for them, and re-layouts: 36.5 us -> 27.5 us  [gather(): jnp.concatenate([block, swap(block, axis, self.sizes[axis], mask)], axis=0)]
    another operation x0 -> x13, local copies, waits for them, and re-layouts: none -> 6.51 us  [the longest x3 2.42 us: gather(): jnp.stack([flat.reshape(self.rows, -1, 2, self.run) for flat in (gate, up...]
    unnamed x152 -> x127, local copies, waits for them, and re-layouts: 25.4 us -> 20.4 us
    concatenate x12 -> x11, other arithmetic: 18.4 us -> 13.5 us  [gather(): jnp.concatenate([block, swap(block, axis, self.sizes[axis], mask)], axis=0)]
    ppermute x46 -> x53, starting transfers between devices: 52.9 us -> 53.5 us  [swap(): lax.ppermute(values, axis, [(index, index ^ mask) for index in range(size)])]
  transfers between devices with their start and end apart: 46 -> 53, of which waited for: 14 -> 22; matrix products, arithmetic and copies ran while one was open for 35% -> 35% of each run, Pallas kernels for 0% -> 0%
where the time goes in v2:
time: 518 us; the launch traced here: 509 us
  waiting for transfers between devices  216 us (42%)
  local copies, waits for them, and re-layouts  102 us (20%)
  matrix products  87.1 us (17%)
  starting transfers between devices  53.5 us (10%)
  other arithmetic  39.6 us (8%)
  blocking collectives  8.74 us (2%)
    ppermute x53, waiting for transfers between devices, swap(): lax.ppermute(values, axis, [(index, index ^ mask) for index in range(size)])  216 us
    ppermute x53, starting transfers between devices, swap(): lax.ppermute(values, axis, [(index, index ^ mask) for index in range(size)])  53.5 us
    dot_general x5, matrix products, batched(): return jnp.einsum(pattern, left, right, preferred_element_type=jnp.float32)  27.8 us
    concatenate x9, local copies, waits for them, and re-layouts, gather(): jnp.concatenate([block, swap(block, axis, self.sizes[axis], mask)], axis=0)  27.5 us
    unnamed x127, local copies, waits for them, and re-layouts  20.4 us
    dot_general x10, matrix products, product_right(): lax.dot_general(left, right, (((1,), (1,)), ((), ())), preferred_element_...  17.3 us
    dot_general x7, matrix products, product(): return jnp.dot(left, right, preferred_element_type=jnp.float32)  15.3 us
    dot_general x7, matrix products, product_left(): lax.dot_general(left, right, (((0,), (0,)), ((), ())), preferred_element_...  14.4 us
  transfers between devices with their start and end apart: 53, of which 22 were waited for; matrix products, arithmetic and copies ran while one was open for 35% of the time, Pallas kernels for 0%

profile of v2, /device:TPU:0, one launch (start us, length us, event | category | flops | bytes accessed | tf_op | source)
XLA Modules:
  0.0 509.1 jit_solution(9818122158251764349)
XLA Ops:
  3.4 4.1 collective-permute-start
  23.8 8.7 %all-gather = bf16[8,120,2]{1,2,0:T(2,128)(2,1)S(1)} all-gather(bf16[1,120,2]{1,2,0:T(2,128)(2,1)S(1)} %bitcast.144), channel_id=1, replica_groups=mesh['dp'=8,'ctx'=4] {'dp'}, dimensions={0}, use_global_device_ids=true | all-gather | bytes 4320 | tf_op jit(solution)/shard_map/all_gather | solution.py:292
  49.9 8.2 %collective-permute-done.1 = bf16[64,1600]{1,0:T(8,128)(2,1)S(1)} collective-permute-done((bf16[64,1600]{1,0:T(8,128)(2,1)}, bf16[64,1600]{1,0:T(8,128)(2,1)S(1)}, u32[]{:S(2)}, u32[]{:S(2)}) %collective-permute-start.1) | collective-permute-done | bytes 204832 | tf_op jit(solution)/shard_map/ppermute | solution.py:40
  86.7 4.5 collective-permute-done.3
  95.3 7.2 %collective-permute-done.11 = bf16[256,960]{1,0:T(8,128)(2,1)} collective-permute-done((bf16[256,960]{1,0:T(8,128)(2,1)}, bf16[256,960]{1,0:T(8,128)(2,1)}, u32[]{:S(2)}, u32[]{:S(2)}) %collective-permute-start.11) | collective-permute-done | bytes 491552 | tf_op jit(solution)/shard_map/ppermute | solution.py:40
  121.4 9.2 %collective-permute-done.17 = bf16[256,2560]{1,0:T(8,128)(2,1)} collective-permute-done((bf16[256,2560]{1,0:T(8,128)(2,1)}, bf16[256,2560]{1,0:T(8,128)(2,1)}, u32[]{:S(2)}, u32[]{:S(2)}) %collective-permute-start.17) | collective-permute-done | bytes 1310752 | tf_op jit(solution)/shard_map/ppermute | solution.py:40
  135.1 7.0 %concatenate.118 = bf16[1024,1600]{0,1:T(8,128)(2,1)} concatenate(bf16[32,1600]{0,1:T(8,128)(2,1)S(1)} %copy.98, bf16[32,1600]{0,1:T(8,128)(2,1)S(1)} %copy.99, bf16[64,1600]{0,1:T(8,128)(2,1)} %copy-done.12, bf16[128,1600]{0,1:T(8,128)(2,1)} %copy-done.13, bf16[256,1600]{0,1:T(8,128)(2,1)} %copy-done.14, bf16[512,1600]{0,1:T(8,128)(2,1)} %collective-permute-done.4), dimensions={0} | concatenate | bytes 6553600 | tf_op jit(solution)/shard_map/concatenate | solution.py:60
  151.6 7.1 %collective-permute-done.7 = bf16[256,640]{0,1:T(8,128)(2,1)S(1)} collective-permute-done((bf16[256,640]{0,1:T(8,128)(2,1)S(1)}, bf16[256,640]{0,1:T(8,128)(2,1)S(1)}, u32[]{:S(2)}, u32[]{:S(2)}) %collective-permute-start.7) | collective-permute-done | bytes 327712 | tf_op jit(solution)/shard_map/ppermute | solution.py:40
  158.6 14.4 %collective-permute-done.6 = bf16[256,640]{0,1:T(8,128)(2,1)S(1)} collective-permute-done((bf16[256,640]{0,1:T(8,128)(2,1)S(1)}, bf16[256,640]{0,1:T(8,128)(2,1)S(1)}, u32[]{:S(2)}, u32[]{:S(2)}) %collective-permute-start.6) | collective-permute-done | bytes 327712 | tf_op jit(solution)/shard_map/ppermute | solution.py:40
  174.2 12.4 %fusion.92 = (f32[5,768]{1,0:T(8,128)S(1)}, f32[5,768,1024]{2,1,0:T(8,128)}) fusion(pred[768,1024]{1,0:T(8,128)(4,1)} %broadcast_compare_fusion, bf16[5,768,64]{1,2,0:T(8,128)(2,1)} %bitcast.118, bf16[5,1024,64]{1,2,0:T(8,128)(2,1)} %bitcast.112), kind=kOutput, calls=%fused_computation.258 | convolution fusion | flops 519046144 | bytes 17677312 | tf_op jit(solution)/shard_map/sub | solution.py:335
  186.6 9.1 %fusion.93 = (bf16[5,768,64]{1,2,0:T(8,128)(2,1)}, f32[5,768,64]{1,2,0:T(8,128)}) fusion(bf16[5,1024,64]{1,2,0:T(8,128)(2,1)S(1)} %bitcast.107, f32[5,768,1024]{2,1,0:T(8,128)} %get-tuple-element.88, f32[5,768]{1,0:T(8,128)S(1)} %broadcast_divide_fusion), kind=kOutput, calls=%fused_computation.259 | convolution fusion | flops 511426560 | bytes 17873920 | tf_op jit(solution)/shard_map/gqk,gkd->gqd/dot_general | solution.py:326
  202.3 4.0 gather_fusion.1
  212.2 3.8 constant_dynamic-update-slice_fusion.12
  216.0 4.8 fusion.95
  227.2 4.6 copy.112
  231.8 4.1 gather_fusion.2
  239.5 5.5 %multiply_convert_fusion.5 = (bf16[512,1280]{1,0:T(8,128)(2,1)S(1)}, bf16[512,1280]{1,0:T(8,128)(2,1)S(1)}) fusion(f32[512,2560]{1,0:T(8,128)S(1)} %copy-done.6, bf16[512,960]{0,1:T(8,128)(2,1)} %constant_dynamic-update-slice_fusion.23, bf16[1280,960]{1,0:T(8,128)(2,1)} %bitcast.116), kind=kOutput, calls=%fused_computation.35 | convolution fusion | flops 1266810880 | bytes 11304960 | tf_op jit(solution)/shard_map/dot_general | solution.py:30
  265.5 6.6 %fusion.14 = f32[5,1024,64]{1,2,0:T(8,128)S(1)} fusion(bf16[5,768,64]{1,2,0:T(8,128)(2,1)S(1)} %reshape.398, f32[5,768,1024]{2,1,0:T(8,128)} %get-tuple-element.88, f32[5,768]{1,0:T(8,128)S(1)} %broadcast_divide_fusion), kind=kOutput, calls=%fused_computation.28 | convolution fusion | flops 511180800 | bytes 17546240 | tf_op jit(solution)/shard_map/gqk,gqd->gkd/dot_general | solution.py:326
  272.3 7.0 %multiply_convert_fusion = bf16[5,768,1024]{2,1,0:T(8,128)(2,1)S(1)} fusion(f32[5,768,1024]{2,1,0:T(8,128)} %get-tuple-element.88, bf16[5,768,64]{1,2,0:T(8,128)(2,1)S(1)} %reshape.398, bf16[5,1024,64]{1,2,0:T(8,128)(2,1)S(1)} %bitcast.108, f32[5,768]{1,0:T(8,128)S(1)} %multiply_reduce_fusion.1, f32[5,768]{1,0:T(8,128)S(1)} %broadcast_divide_fusion), kind=kOutput, calls=%fused_computation.4 | convolution fusion | flops 519045120 | bytes 24770560 | tf_op jit(solution)/shard_map/gqd,gkd->gqk/dot_general | solution.py:326
  293.4 7.9 %collective-permute-done.28 = bf16[256,640]{0,1:T(8,128)(2,1)S(1)} collective-permute-done((bf16[256,640]{0,1:T(8,128)(2,1)S(1)}, bf16[256,640]{0,1:T(8,128)(2,1)S(1)}, u32[]{:S(2)}, u32[]{:S(2)}) %collective-permute-start.28) | collective-permute-done | bytes 327712 | tf_op jit(solution)/shard_map/ppermute | solution.py:40
  301.2 8.6 %collective-permute-done.26 = bf16[256,640]{0,1:T(8,128)(2,1)S(1)} collective-permute-done((bf16[256,640]{0,1:T(8,128)(2,1)S(1)}, bf16[256,640]{0,1:T(8,128)(2,1)S(1)}, u32[]{:S(2)}, u32[]{:S(2)}) %collective-permute-start.26) | collective-permute-done | bytes 327712 | tf_op jit(solution)/shard_map/ppermute | solution.py:40
  309.8 8.7 %collective-permute-done.27 = bf16[256,640]{0,1:T(8,128)(2,1)S(1)} collective-permute-done((bf16[256,640]{0,1:T(8,128)(2,1)S(1)}, bf16[256,640]{0,1:T(8,128)(2,1)S(1)}, u32[]{:S(2)}, u32[]{:S(2)}) %collective-permute-start.27) | collective-permute-done | bytes 327712 | tf_op jit(solution)/shard_map/ppermute | solution.py:40
  331.6 54.1 %collective-permute-done.49 = f32[2,2,120]{2,1,0:T(2,128)S(1)} collective-permute-done((f32[2,2,120]{2,1,0:T(2,128)S(1)}, f32[2,2,120]{2,1,0:T(2,128)S(1)}, u32[]{:S(2)}, u32[]{:S(2)}) %collective-permute-start.49) | collective-permute-done | bytes 1952 | tf_op jit(solution)/shard_map/ppermute | solution.py:40
  394.1 10.8 %collective-permute-done.45 = bf16[4,80,960]{2,1,0:T(8,128)(2,1)S(1)} collective-permute-done((bf16[4,80,960]{2,1,0:T(8,128)(2,1)S(1)}, bf16[4,80,960]{2,1,0:T(8,128)(2,1)S(1)}, u32[]{:S(2)}, u32[]{:S(2)}) %collective-permute-start.45) | collective-permute-done | bytes 614432 | tf_op jit(solution)/shard_map/ppermute | solution.py:40
  406.7 7.7 %collective-permute-done.46 = bf16[2,80,960]{2,1,0:T(8,128)(2,1)S(1)} collective-permute-done((bf16[2,80,960]{2,1,0:T(8,128)(2,1)S(1)}, bf16[2,80,960]{2,1,0:T(8,128)(2,1)S(1)}, u32[]{:S(2)}, u32[]{:S(2)}) %collective-permute-start.46) | collective-permute-done | bytes 307232 | tf_op jit(solution)/shard_map/ppermute | solution.py:40
  418.8 5.0 collective-permute-done.47
  424.8 4.2 add_convert_fusion
  429.7 7.9 %collective-permute-done.30 = bf16[256,1600]{0,1:T(8,128)(2,1)S(1)} collective-permute-done((bf16[256,1600]{0,1:T(8,128)(2,1)}, bf16[256,1600]{0,1:T(8,128)(2,1)S(1)}, u32[]{:S(2)}, u32[]{:S(2)}) %collective-permute-start.30) | collective-permute-done | bytes 819232 | tf_op jit(solution)/shard_map/ppermute | solution.py:40
  441.6 4.3 collective-permute-done.31
  448.7 14.7 %collective-permute-done.40 = bf16[256,2560]{1,0:T(8,128)(2,1)S(1)} collective-permute-done((bf16[256,2560]{1,0:T(8,128)(2,1)S(1)}, bf16[256,2560]{1,0:T(8,128)(2,1)S(1)}, u32[]{:S(2)}, u32[]{:S(2)}) %collective-permute-start.40) | collective-permute-done | bytes 1310752 | tf_op jit(solution)/shard_map/ppermute | solution.py:40
  471.0 15.9 %collective-permute-done.41 = bf16[128,2560]{1,0:T(8,128)(2,1)S(1)} collective-permute-done((bf16[128,2560]{1,0:T(8,128)(2,1)S(1)}, bf16[128,2560]{1,0:T(8,128)(2,1)S(1)}, u32[]{:S(2)}, u32[]{:S(2)}) %collective-permute-start.41) | collective-permute-done | bytes 655392 | tf_op jit(solution)/shard_map/ppermute | solution.py:40
  488.8 13.9 %collective-permute-done.42 = bf16[64,2560]{1,0:T(8,128)(2,1)S(1)} collective-permute-done((bf16[64,2560]{1,0:T(8,128)(2,1)S(1)}, bf16[64,2560]{1,0:T(8,128)(2,1)S(1)}, u32[]{:S(2)}, u32[]{:S(2)}) %collective-permute-start.42) | collective-permute-done | bytes 327712 | tf_op jit(solution)/shard_map/ppermute | solution.py:40
  (421 shorter events, 210.8 us)
Async XLA Ops:
  3.4 38.7 %collective-permute-start = (bf16[32,1600]{1,0:T(8,128)(2,1)S(1)}, bf16[32,1600]{1,0:T(8,128)(2,1)S(1)}, u32[]{:S(2)}, u32[]{:S(2)}) collective-permute-start(bf16[32,1600]{1,0:T(8,128)(2,1)S(1)} %pad.15), channel_id=1, source_target_pairs={{0,2},{1,3},{2,0},{3,1},{4,6},{5,7},{6,4},{7,5},{8,10},{9,11},{10,... | collective-permute-start | bytes 307208 | tf_op jit(solution)/shard_map/ppermute | solution.py:40
  8.5 34.9 %collective-permute-start.19 = (bf16[1,80,960]{2,1,0:T(8,128)(2,1)S(1)}, bf16[1,80,960]{2,1,0:T(8,128)(2,1)S(1)}, u32[]{:S(2)}, u32[]{:S(2)}) collective-permute-start(bf16[1,80,960]{2,1,0:T(8,128)(2,1)S(1)} %reshape.394), channel_id=1, source_target_pairs={{0,2},{1,3},{2,0},{3,1},{4,6},{5,7},{6,4},{7,5},{8,10},{9,11},{10,... | collective-permute-start | bytes 460808 | tf_op jit(solution)/shard_map/ppermute | solution.py:40
  8.6 84.7 %collective-permute-start.24 = (bf16[256,960]{0,1:T(8,128)(2,1)}, bf16[256,960]{0,1:T(8,128)(2,1)}, u32[]{:S(2)}, u32[]{:S(2)}) collective-permute-start(bf16[256,960]{0,1:T(8,128)(2,1)} %param.21), channel_id=1, source_target_pairs={{0,4},{4,0},{8,12},{12,8},{16,20},{20,16},{24,28},{28,24},{1,5},{5... | collective-permute-start | bytes 1474568 | tf_op jit(solution)/shard_map/ppermute | solution.py:40
  10.3 28.6 %collective-permute-start.8 = (bf16[32,960]{1,0:T(8,128)(2,1)S(1)}, bf16[32,960]{1,0:T(8,128)(2,1)S(1)}, u32[]{:S(2)}, u32[]{:S(2)}) collective-permute-start(bf16[32,960]{1,0:T(8,128)(2,1)S(1)} %get-tuple-element.75), channel_id=1, source_target_pairs={{0,2},{1,3},{2,0},{3,1},{4,6},{5,7},{6,4},{7,5},{8,10},{9,11},{10,... | collective-permute-start | bytes 184328 | tf_op jit(solution)/shard_map/ppermute | solution.py:40
  17.6 28.9 %collective-permute-start.14 = (bf16[32,2560]{1,0:T(8,128)(2,1)S(1)}, bf16[32,2560]{1,0:T(8,128)(2,1)S(1)}, u32[]{:S(2)}, u32[]{:S(2)}) collective-permute-start(bf16[32,2560]{1,0:T(8,128)(2,1)S(1)} %get-tuple-element.69), channel_id=1, source_target_pairs={{0,4},{4,0},{8,12},{12,8},{16,20},{20,16},{24,28},{28,24},{1,5},{5... | collective-permute-start | bytes 491528 | tf_op jit(solution)/shard_map/ppermute | solution.py:40
  44.2 32.9 %collective-permute-start.20 = (bf16[2,80,960]{2,1,0:T(8,128)(2,1)}, bf16[2,80,960]{2,1,0:T(8,128)(2,1)}, u32[]{:S(2)}, u32[]{:S(2)}) collective-permute-start(bf16[2,80,960]{2,1,0:T(8,128)(2,1)} %pad_maximum_fusion.15), channel_id=1, source_target_pairs={{0,1},{1,0},{2,3},{3,2},{4,5},{5,4},{6,7},{7,6},{8,9},{9,8},{10,11... | collective-permute-start | bytes 921608 | tf_op jit(solution)/shard_map/ppermute | solution.py:40
  48.4 22.9 %collective-permute-start.10 = (bf16[128,960]{1,0:T(8,128)(2,1)}, bf16[128,960]{1,0:T(8,128)(2,1)}, u32[]{:S(2)}, u32[]{:S(2)}) collective-permute-start(bf16[128,960]{1,0:T(8,128)(2,1)} %pad_maximum_fusion.16), channel_id=1, source_target_pairs={{0,8},{4,12},{8,0},{12,4},{16,24},{20,28},{24,16},{28,20},{1,9},{5... | collective-permute-start | bytes 737288 | tf_op jit(solution)/shard_map/ppermute | solution.py:40
  63.4 17.1 %collective-permute-start.16 = (bf16[128,2560]{1,0:T(8,128)(2,1)}, bf16[128,2560]{1,0:T(8,128)(2,1)}, u32[]{:S(2)}, u32[]{:S(2)}) collective-permute-start(bf16[128,2560]{1,0:T(8,128)(2,1)} %pad_maximum_fusion.6), channel_id=1, source_target_pairs={{0,1},{1,0},{2,3},{3,2},{4,5},{5,4},{6,7},{7,6},{8,9},{9,8},{10,11... | collective-permute-start | bytes 1966088 | tf_op jit(solution)/shard_map/ppermute | solution.py:40
  69.8 21.4 %collective-permute-start.3 = (bf16[256,1600]{0,1:T(8,128)(2,1)}, bf16[256,1600]{0,1:T(8,128)(2,1)S(1)}, u32[]{:S(2)}, u32[]{:S(2)}) collective-permute-start(bf16[256,1600]{0,1:T(8,128)(2,1)} %copy.93), channel_id=1, source_target_pairs={{0,16},{4,20},{8,24},{12,28},{16,0},{20,4},{24,8},{28,12},{1,17},{... | collective-permute-start | bytes 2457608 | tf_op jit(solution)/shard_map/ppermute | solution.py:40
  73.1 29.4 %collective-permute-start.11 = (bf16[256,960]{1,0:T(8,128)(2,1)}, bf16[256,960]{1,0:T(8,128)(2,1)}, u32[]{:S(2)}, u32[]{:S(2)}) collective-permute-start(bf16[256,960]{1,0:T(8,128)(2,1)} %pad_maximum_fusion.8), channel_id=1, source_target_pairs={{0,16},{4,20},{8,24},{12,28},{16,0},{20,4},{24,8},{28,12},{1,17},{... | collective-permute-start | bytes 1474568 | tf_op jit(solution)/shard_map/ppermute | solution.py:40
  79.0 30.6 %collective-permute-start.21 = (bf16[4,80,960]{2,1,0:T(8,128)(2,1)}, bf16[4,80,960]{2,1,0:T(8,128)(2,1)}, u32[]{:S(2)}, u32[]{:S(2)}) collective-permute-start(bf16[4,80,960]{2,1,0:T(8,128)(2,1)} %pad_maximum_fusion.7), channel_id=1, source_target_pairs={{0,8},{4,12},{8,0},{12,4},{16,24},{20,28},{24,16},{28,20},{1,9},{5... | collective-permute-start | bytes 1843208 | tf_op jit(solution)/shard_map/ppermute | solution.py:40
  82.8 47.8 %collective-permute-start.17 = (bf16[256,2560]{1,0:T(8,128)(2,1)}, bf16[256,2560]{1,0:T(8,128)(2,1)}, u32[]{:S(2)}, u32[]{:S(2)}) collective-permute-start(bf16[256,2560]{1,0:T(8,128)(2,1)} %pad_maximum_fusion.2), channel_id=1, source_target_pairs={{0,16},{4,20},{8,24},{12,28},{16,0},{20,4},{24,8},{28,12},{1,17},{... | collective-permute-start | bytes 3932168 | tf_op jit(solution)/shard_map/ppermute | solution.py:40
  93.4 41.7 %collective-permute-start.4 = (bf16[512,1600]{0,1:T(8,128)(2,1)}, bf16[512,1600]{0,1:T(8,128)(2,1)}, u32[]{:S(2)}, u32[]{:S(2)}) collective-permute-start(bf16[512,1600]{0,1:T(8,128)(2,1)} %concatenate.117), channel_id=1, source_target_pairs={{0,4},{4,0},{8,12},{12,8},{16,20},{20,16},{24,28},{28,24},{1,5},{5... | collective-permute-start | bytes 4915208 | tf_op jit(solution)/shard_map/ppermute | solution.py:40
  112.0 87.9 %collective-permute-start.22 = (bf16[8,80,960]{2,1,0:T(8,128)(2,1)}, bf16[8,80,960]{2,1,0:T(8,128)(2,1)}, u32[]{:S(2)}, u32[]{:S(2)}) collective-permute-start(bf16[8,80,960]{2,1,0:T(8,128)(2,1)} %pad_maximum_fusion.3), channel_id=1, source_target_pairs={{0,16},{4,20},{8,24},{12,28},{16,0},{20,4},{24,8},{28,12},{1,17},{... | collective-permute-start | bytes 3686408 | tf_op jit(solution)/shard_map/ppermute | solution.py:40
  133.6 78.7 %collective-permute-start.18 = (bf16[512,2560]{1,0:T(8,128)(2,1)}, bf16[512,2560]{1,0:T(8,128)(2,1)}, u32[]{:S(2)}, u32[]{:S(2)}) collective-permute-start(bf16[512,2560]{1,0:T(8,128)(2,1)} %get-tuple-element.44), channel_id=1, source_target_pairs={{0,8},{4,12},{8,0},{12,4},{16,24},{20,28},{24,16},{28,20},{1,9},{5... | collective-permute-start | bytes 7864328 | tf_op jit(solution)/shard_map/ppermute | solution.py:40
  148.9 24.1 %collective-permute-start.6 = (bf16[256,640]{0,1:T(8,128)(2,1)S(1)}, bf16[256,640]{0,1:T(8,128)(2,1)S(1)}, u32[]{:S(2)}, u32[]{:S(2)}) collective-permute-start(bf16[256,640]{0,1:T(8,128)(2,1)S(1)} %pad_maximum_fusion.13), channel_id=1, source_target_pairs={{0,2},{1,3},{2,0},{3,1},{4,6},{5,7},{6,4},{7,5},{8,10},{9,11},{10,... | collective-permute-start | bytes 983048 | tf_op jit(solution)/shard_map/ppermute | solution.py:40
  148.9 24.1 %collective-permute-start.5 = (bf16[256,640]{0,1:T(8,128)(2,1)S(1)}, bf16[256,640]{0,1:T(8,128)(2,1)S(1)}, u32[]{:S(2)}, u32[]{:S(2)}) collective-permute-start(bf16[256,640]{0,1:T(8,128)(2,1)S(1)} %pad_maximum_fusion.13), channel_id=1, source_target_pairs={{0,1},{1,0},{2,3},{3,2},{4,5},{5,4},{6,7},{7,6},{8,9},{9,8},{10,11... | collective-permute-start | bytes 983048 | tf_op jit(solution)/shard_map/ppermute | solution.py:40
  257.8 128.0 %collective-permute-start.44 = (bf16[8,80,960]{2,1,0:T(8,128)(2,1)}, bf16[8,80,960]{2,1,0:T(8,128)(2,1)}, u32[]{:S(2)}, u32[]{:S(2)}) collective-permute-start(bf16[8,80,960]{2,1,0:T(8,128)(2,1)} %slice.329), channel_id=1, source_target_pairs={{0,16},{4,20},{8,24},{12,28},{16,0},{20,4},{24,8},{28,12},{1,17},{... | collective-permute-start | bytes 3686408 | tf_op jit(solution)/shard_map/ppermute | solution.py:40
  291.4 18.4 %collective-permute-start.26 = (bf16[256,640]{0,1:T(8,128)(2,1)S(1)}, bf16[256,640]{0,1:T(8,128)(2,1)S(1)}, u32[]{:S(2)}, u32[]{:S(2)}) collective-permute-start(bf16[256,640]{0,1:T(8,128)(2,1)S(1)} %bitcast.132), channel_id=1, source_target_pairs={{0,1},{1,0},{2,3},{3,2},{4,5},{5,4},{6,7},{7,6},{8,9},{9,8},{10,11... | collective-permute-start | bytes 983048 | tf_op jit(solution)/shard_map/ppermute | solution.py:40
  291.4 27.0 %collective-permute-start.27 = (bf16[256,640]{0,1:T(8,128)(2,1)S(1)}, bf16[256,640]{0,1:T(8,128)(2,1)S(1)}, u32[]{:S(2)}, u32[]{:S(2)}) collective-permute-start(bf16[256,640]{0,1:T(8,128)(2,1)S(1)} %bitcast.131), channel_id=1, source_target_pairs={{0,2},{1,3},{2,0},{3,1},{4,6},{5,7},{6,4},{7,5},{8,10},{9,11},{10,... | collective-permute-start | bytes 983048 | tf_op jit(solution)/shard_map/ppermute | solution.py:40
  328.0 96.8 %collective-permute-start.39 = (bf16[512,2560]{1,0:T(8,128)(2,1)}, bf16[512,2560]{1,0:T(8,128)(2,1)}, u32[]{:S(2)}, u32[]{:S(2)}) collective-permute-start(bf16[512,2560]{1,0:T(8,128)(2,1)} %convolution_convert_fusion), channel_id=1, source_target_pairs={{0,8},{4,12},{8,0},{12,4},{16,24},{20,28},{24,16},{28,20},{1,9},{5... | collective-permute-start | bytes 7864328 | tf_op jit(solution)/shard_map/ppermute | solution.py:40
  328.5 63.5 %collective-permute-start.34 = (bf16[512,960]{0,1:T(8,128)(2,1)}, bf16[512,960]{0,1:T(8,128)(2,1)S(1)}, u32[]{:S(2)}, u32[]{:S(2)}) collective-permute-start(bf16[512,960]{0,1:T(8,128)(2,1)} %convolution_convert_fusion.3), channel_id=1, source_target_pairs={{0,4},{4,0},{8,12},{12,8},{16,20},{20,16},{24,28},{28,24},{1,5},{5... | collective-permute-start | bytes 2949128 | tf_op jit(solution)/shard_map/ppermute | solution.py:40
  330.1 55.6 %collective-permute-start.49 = (f32[2,2,120]{2,1,0:T(2,128)S(1)}, f32[2,2,120]{2,1,0:T(2,128)S(1)}, u32[]{:S(2)}, u32[]{:S(2)}) collective-permute-start(f32[2,2,120]{2,1,0:T(2,128)S(1)} %slice.427), channel_id=1, source_target_pairs={{0,8},{4,12},{8,0},{12,4},{16,24},{20,28},{24,16},{28,20},{1,9},{5... | collective-permute-start | bytes 5768 | tf_op jit(solution)/shard_map/ppermute | solution.py:40
  331.6 83.0 %collective-permute-start.29 = (bf16[512,1600]{0,1:T(8,128)(2,1)}, bf16[512,1600]{0,1:T(8,128)(2,1)S(1)}, u32[]{:S(2)}, u32[]{:S(2)}) collective-permute-start(bf16[512,1600]{0,1:T(8,128)(2,1)} %convolution_convert_fusion.2), channel_id=1, source_target_pairs={{0,4},{4,0},{8,12},{12,8},{16,20},{20,16},{24,28},{28,24},{1,5},{5... | collective-permute-start | bytes 4915208 | tf_op jit(solution)/shard_map/ppermute | solution.py:40
  387.9 17.0 %collective-permute-start.45 = (bf16[4,80,960]{2,1,0:T(8,128)(2,1)S(1)}, bf16[4,80,960]{2,1,0:T(8,128)(2,1)S(1)}, u32[]{:S(2)}, u32[]{:S(2)}) collective-permute-start(bf16[4,80,960]{2,1,0:T(8,128)(2,1)S(1)} %slice.419), channel_id=1, source_target_pairs={{0,8},{4,12},{8,0},{12,4},{16,24},{20,28},{24,16},{28,20},{1,9},{5... | collective-permute-start | bytes 1843208 | tf_op jit(solution)/shard_map/ppermute | solution.py:40
  416.2 21.4 %collective-permute-start.30 = (bf16[256,1600]{0,1:T(8,128)(2,1)}, bf16[256,1600]{0,1:T(8,128)(2,1)S(1)}, u32[]{:S(2)}, u32[]{:S(2)}) collective-permute-start(bf16[256,1600]{0,1:T(8,128)(2,1)} %slice.382), channel_id=1, source_target_pairs={{0,16},{4,20},{8,24},{12,28},{16,0},{20,4},{24,8},{28,12},{1,17},{... | collective-permute-start | bytes 2457608 | tf_op jit(solution)/shard_map/ppermute | solution.py:40
  417.0 21.5 %collective-permute-start.37 = (bf16[64,960]{0,1:T(8,128)(2,1)S(1)}, bf16[64,960]{0,1:T(8,128)(2,1)S(1)}, u32[]{:S(2)}, u32[]{:S(2)}) collective-permute-start(bf16[64,960]{0,1:T(8,128)(2,1)S(1)} %slice.398), channel_id=1, source_target_pairs={{0,1},{1,0},{2,3},{3,2},{4,5},{5,4},{6,7},{7,6},{8,9},{9,8},{10,11... | collective-permute-start | bytes 368648 | tf_op jit(solution)/shard_map/ppermute | solution.py:40
  429.1 34.2 %collective-permute-start.40 = (bf16[256,2560]{1,0:T(8,128)(2,1)S(1)}, bf16[256,2560]{1,0:T(8,128)(2,1)S(1)}, u32[]{:S(2)}, u32[]{:S(2)}) collective-permute-start(bf16[256,2560]{1,0:T(8,128)(2,1)S(1)} %slice.405), channel_id=1, source_target_pairs={{0,16},{4,20},{8,24},{12,28},{16,0},{20,4},{24,8},{28,12},{1,17},{... | collective-permute-start | bytes 3932168 | tf_op jit(solution)/shard_map/ppermute | solution.py:40
  438.7 26.5 %collective-permute-start.38 = (bf16[32,960]{0,1:T(8,128)(2,1)S(1)}, bf16[32,960]{0,1:T(8,128)(2,1)S(1)}, u32[]{:S(2)}, u32[]{:S(2)}) collective-permute-start(bf16[32,960]{0,1:T(8,128)(2,1)S(1)} %get-tuple-element.71), channel_id=1, source_target_pairs={{0,2},{1,3},{2,0},{3,1},{4,6},{5,7},{6,4},{7,5},{8,10},{9,11},{10,... | collective-permute-start | bytes 184328 | tf_op jit(solution)/shard_map/ppermute | solution.py:40
  447.0 20.8 %collective-permute-start.32 = (bf16[64,1600]{0,1:T(8,128)(2,1)}, bf16[64,1600]{0,1:T(8,128)(2,1)}, u32[]{:S(2)}, u32[]{:S(2)}) collective-permute-start(bf16[64,1600]{0,1:T(8,128)(2,1)} %slice.386), channel_id=1, source_target_pairs={{0,1},{1,0},{2,3},{3,2},{4,5},{5,4},{6,7},{7,6},{8,9},{9,8},{10,11... | collective-permute-start | bytes 614408 | tf_op jit(solution)/shard_map/ppermute | solution.py:40
  463.7 23.2 %collective-permute-start.41 = (bf16[128,2560]{1,0:T(8,128)(2,1)S(1)}, bf16[128,2560]{1,0:T(8,128)(2,1)S(1)}, u32[]{:S(2)}, u32[]{:S(2)}) collective-permute-start(bf16[128,2560]{1,0:T(8,128)(2,1)S(1)} %slice.407), channel_id=1, source_target_pairs={{0,1},{1,0},{2,3},{3,2},{4,5},{5,4},{6,7},{7,6},{8,9},{9,8},{10,11... | collective-permute-start | bytes 1966088 | tf_op jit(solution)/shard_map/ppermute | solution.py:40
  469.1 18.6 %collective-permute-start.33 = (bf16[32,1600]{0,1:T(8,128)(2,1)S(1)}, bf16[32,1600]{0,1:T(8,128)(2,1)S(1)}, u32[]{:S(2)}, u32[]{:S(2)}) collective-permute-start(bf16[32,1600]{0,1:T(8,128)(2,1)S(1)} %slice.388), channel_id=1, source_target_pairs={{0,2},{1,3},{2,0},{3,1},{4,6},{5,7},{6,4},{7,5},{8,10},{9,11},{10,... | collective-permute-start | bytes 307208 | tf_op jit(solution)/shard_map/ppermute | solution.py:40
  (78 other events, 732.2 us)
